TPU v7x, 768 devices: a whole 4x8x12 slice. The times are simulated.
768 devices in a mesh: group: 12 (over z_lo, core), blk: 64 (over y, x, z_hi).
Axes of the slice: x: 4, y: 8, z: 12 (z_hi: 2, z_lo: 6; z = z_hi * 6 + z_lo), core: 2. Of those that a mesh axis runs over, the one named last changes fastest.
Arguments:
- image_embed: bfloat16 [294912, 1024], P(('group', 'blk')), may hold values from -0.25 to 0.25
- text_embed: bfloat16 [294912, 1024], P(('group', 'blk')), may hold values from -0.25 to 0.25
- positive_partner_index: int32 [294912], P(('group', 'blk')), may hold values from 0 to 294911, as said below
- exponent_of_multiplier: float32 [1], replicated, may hold values from 1 to 2
- logit_bias: float32 [1], replicated, may hold values from -4 to -1
Outputs:
- image_grad: float32 [294912, 1024], P(('group', 'blk'))
- text_grad: float32 [294912, 1024], P(('group', 'blk'))
Inputs may be any that keep to these rules, and one draw needn't show every extreme that they name: `positive_partner_index`: each row names a row of one of the four text blocks that its image block is scored against.
All inputs are finite; a program needn't handle non-finite values.
Results may differ from a plain program's by a relative error of at most 0.0039.
Values may be sent and summed in bfloat16 or wider, within the bound.
No kernel may reach another device: no remote copies, remote signals or barrier semaphores. Data moves between devices by JAX's collectives and lax.ppermute only.
A program may use at most 32 MiB of HBM per device.

v0:
```python
import jax
import jax.numpy as jnp
from jax import lax
from jax.sharding import PartitionSpec as P


def from_behind(array, axis, by):
    count = lax.axis_size(axis)
    return lax.ppermute(array, axis, [(i, (i + by) % count) for i in range(count)])


def normalize(values):
    wide = values.astype(jnp.float32)
    norms = jnp.sqrt(jnp.sum(wide * wide, axis=-1, keepdims=True) + 1e-06)
    return (wide / norms, norms)


def back_through(unit, norms, grad):
    return (grad - unit * jnp.sum(unit * grad, axis=-1, keepdims=True)) / norms


def block_label_sign(
    leading_unitlength,
    latter_unitlength,
    matching_entry_position,
    leading_field_position,
    affinity_multiplier,
    trainable_offset_term,
):
    affinity_matrix = (
        affinity_multiplier
        * lax.dot_general(
            leading_unitlength,
            latter_unitlength,
            (((1,), (1,)), ((), ())),
            preferred_element_type=jnp.float32,
        )
        + trainable_offset_term
    )
    columns = leading_field_position + jnp.arange(latter_unitlength.shape[0])
    labels = jnp.where(matching_entry_position[:, None] == columns[None, :], 1.0, -1.0).astype(
        jnp.float32
    )
    return (-labels * jax.nn.sigmoid(-labels * affinity_matrix)).astype(jnp.bfloat16)


def leading_phrase_vectors(target_polarity, latter_unitlength, affinity_multiplier):
    return affinity_multiplier * jnp.dot(
        target_polarity, latter_unitlength, preferred_element_type=jnp.float32
    )


def latter_phrase_vectors(target_polarity, leading_unitlength, affinity_multiplier):
    return affinity_multiplier * lax.dot_general(
        target_polarity,
        leading_unitlength,
        (((0,), (0,)), ((), ())),
        preferred_element_type=jnp.float32,
    )


def per_device(image_embed, text_embed, positive_partner_index, exponent_of_multiplier, logit_bias):
    affinity_multiplier = jnp.exp(exponent_of_multiplier[0])
    trainable_offset_term = logit_bias[0]
    leading_unitlength, image_norm = normalize(image_embed)
    latter_unitlength, text_norm = normalize(text_embed)
    leading_cyclic_offset = leading_unitlength.astype(jnp.bfloat16)
    latter_cyclic_offset = latter_unitlength.astype(jnp.bfloat16)
    cycle_size = lax.axis_size("blk")
    group_count = lax.axis_size("group")
    local_rows = image_embed.shape[0]
    group_pos = lax.axis_index("group")
    cycle_pos = lax.axis_index("blk")

    def first_of(group_at, cycle_at):
        return (group_at * cycle_size + cycle_at) * local_rows

    local_first_rows = first_of(group_pos, cycle_pos)
    adjacent_first_rows = first_of(group_pos, (cycle_pos + cycle_size - 1) % cycle_size)
    distant_first_rows = first_of(group_pos, (cycle_pos + cycle_size - 2) % cycle_size)
    across_first_rows = first_of((group_pos + group_count - 1) % group_count, cycle_pos)
    nearby_latter_vectors = from_behind(latter_cyclic_offset, "blk", 1)
    remote_latter_vectors = from_behind(latter_cyclic_offset, "blk", 2)
    crosswise_latter_vectors = from_behind(latter_cyclic_offset, "group", 1)
    onsite_target_polarity = block_label_sign(
        leading_cyclic_offset,
        latter_cyclic_offset,
        positive_partner_index,
        local_first_rows,
        affinity_multiplier,
        trainable_offset_term,
    )
    nearby_target_polarity = block_label_sign(
        leading_cyclic_offset,
        nearby_latter_vectors,
        positive_partner_index,
        adjacent_first_rows,
        affinity_multiplier,
        trainable_offset_term,
    )
    remote_target_polarity = block_label_sign(
        leading_cyclic_offset,
        remote_latter_vectors,
        positive_partner_index,
        distant_first_rows,
        affinity_multiplier,
        trainable_offset_term,
    )
    crosswise_target_polarity = block_label_sign(
        leading_cyclic_offset,
        crosswise_latter_vectors,
        positive_partner_index,
        across_first_rows,
        affinity_multiplier,
        trainable_offset_term,
    )
    normalized_first_gradient = leading_phrase_vectors(
        onsite_target_polarity, latter_cyclic_offset, affinity_multiplier
    ) + leading_phrase_vectors(nearby_target_polarity, nearby_latter_vectors, affinity_multiplier)
    normalized_first_gradient = (
        normalized_first_gradient
        + leading_phrase_vectors(remote_target_polarity, remote_latter_vectors, affinity_multiplier)
        + leading_phrase_vectors(
            crosswise_target_polarity, crosswise_latter_vectors, affinity_multiplier
        )
    )
    onsite_latter_vectors = latter_phrase_vectors(
        onsite_target_polarity, leading_cyclic_offset, affinity_multiplier
    )
    adjacent_partition = latter_phrase_vectors(
        nearby_target_polarity, leading_cyclic_offset, affinity_multiplier
    )
    remote_piece = latter_phrase_vectors(
        remote_target_polarity, leading_cyclic_offset, affinity_multiplier
    )
    crosswise_piece = latter_phrase_vectors(
        crosswise_target_polarity, leading_cyclic_offset, affinity_multiplier
    )
    near_back = from_behind(adjacent_partition, "blk", -1)
    far_back = from_behind(remote_piece, "blk", -2)
    cross_back = from_behind(crosswise_piece, "group", -1)
    unit_text_grad = onsite_latter_vectors + near_back + far_back + cross_back
    image_grad = back_through(leading_unitlength, image_norm, normalized_first_gradient)
    text_grad = back_through(latter_unitlength, text_norm, unit_text_grad)
    return (image_grad, text_grad)


def solution(mesh):
    return jax.shard_map(
        per_device,
        mesh=mesh,
        in_specs=(
            P(("group", "blk"), None),
            P(("group", "blk"), None),
            P(("group", "blk")),
            P(),
            P(),
        ),
        out_specs=(P(("group", "blk"), None), P(("group", "blk"), None)),
        check_vma=False,
    )
```

profile of v0, /device:TPU:287, one launch (start us, length us, event | category | flops | bytes accessed | tf_op | source)
XLA Modules:
  0.0 213.0 jit_solution(1760673676863506428)
XLA Ops:
  0.6 0.0 copy-start
  0.6 1.4 fusion.1
  2.1 1.4 fusion.35
  3.5 0.0 copy-start.2
  3.5 4.3 %collective-permute-start.1 = (bf16[384,1024]{1,0:T(8,128)(2,1)S(1)}, bf16[384,1024]{1,0:T(8,128)(2,1)S(1)}, u32[]{:S(2)}, u32[]{:S(2)}) collective-permute-start(bf16[384,1024]{1,0:T(8,128)(2,1)S(1)} %fusion.35), channel_id=1, source_target_pairs={{0,2},{1,3},{2,4},{3,5},{4,6},{5,7},{6,8},{7,9},{8,10},{9,11},{10,... | collective-permute-start | bytes 2359304 | tf_op jit(solution)/shard_map/ppermute | solution.py:9
  7.8 10.7 %collective-permute-start = (bf16[384,1024]{1,0:T(8,128)(2,1)S(1)}, bf16[384,1024]{1,0:T(8,128)(2,1)S(1)}, u32[]{:S(2)}, u32[]{:S(2)}) collective-permute-start(bf16[384,1024]{1,0:T(8,128)(2,1)S(1)} %fusion.35), channel_id=1, source_target_pairs={{0,1},{1,2},{2,3},{3,4},{4,5},{5,6},{6,7},{7,8},{8,9},{9,10},{10,1... | collective-permute-start | bytes 2359304 | tf_op jit(solution)/shard_map/ppermute | solution.py:9
  18.5 3.6 %collective-permute-start.2 = (bf16[384,1024]{1,0:T(8,128)(2,1)S(1)}, bf16[384,1024]{1,0:T(8,128)(2,1)}, u32[]{:S(2)}, u32[]{:S(2)}) collective-permute-start(bf16[384,1024]{1,0:T(8,128)(2,1)S(1)} %fusion.35), channel_id=1, source_target_pairs={{0,64},{64,128},{128,192},{192,256},{256,320},{320,384},{384,448},... | collective-permute-start | bytes 2359304 | tf_op jit(solution)/shard_map/ppermute | solution.py:9
  22.2 0.0 copy-done
  22.2 0.2 fusion
  23.8 0.3 fusion.34
  24.1 0.0 copy-done.2
  24.1 0.7 fusion.33
  24.8 53.1 %collective-permute-done.2 = bf16[384,1024]{1,0:T(8,128)(2,1)} collective-permute-done((bf16[384,1024]{1,0:T(8,128)(2,1)S(1)}, bf16[384,1024]{1,0:T(8,128)(2,1)}, u32[]{:S(2)}, u32[]{:S(2)}) %collective-permute-start.2) | collective-permute-done | bytes 786464 | tf_op jit(solution)/shard_map/ppermute | solution.py:9
  77.9 1.8 fusion.30
  79.8 0.6 convolution_multiply_fusion
  80.4 3.4 %collective-permute-start.5 = (f32[384,1024]{1,0:T(8,128)S(1)}, f32[384,1024]{1,0:T(8,128)S(1)}, u32[]{:S(2)}, u32[]{:S(2)}) collective-permute-start(f32[384,1024]{1,0:T(8,128)S(1)} %convolution_multiply_fusion), channel_id=1, source_target_pairs={{0,704},{64,0},{128,64},{192,128},{256,192},{320,256},{384,320},{4... | collective-permute-start | bytes 4718600 | tf_op jit(solution)/shard_map/ppermute | solution.py:9
  83.8 0.0 collective-permute-done.1
  83.8 0.7 fusion.31
  84.5 0.6 convolution_multiply_fusion.1
  85.1 1.9 collective-permute-start.4
  87.0 0.0 collective-permute-done
  87.1 0.7 fusion.32
  87.8 0.6 convolution_multiply_fusion.2
  88.4 1.9 collective-permute-start.3
  90.3 0.6 fusion.36
  90.9 0.6 fusion.38
  91.5 0.6 fusion.37
  92.0 2.0 multiply_reduce_fusion.1
  94.1 0.0 copy-start.1
  94.1 1.5 subtract_divide_fusion.1
  95.6 76.6 %collective-permute-done.5 = f32[384,1024]{1,0:T(8,128)S(1)} collective-permute-done((f32[384,1024]{1,0:T(8,128)S(1)}, f32[384,1024]{1,0:T(8,128)S(1)}, u32[]{:S(2)}, u32[]{:S(2)}) %collective-permute-start.5) | collective-permute-done | bytes 1572896 | tf_op jit(solution)/shard_map/ppermute | solution.py:9
  172.2 0.0 collective-permute-done.4
  172.2 38.4 %collective-permute-done.3 = f32[384,1024]{1,0:T(8,128)S(1)} collective-permute-done((f32[384,1024]{1,0:T(8,128)S(1)}, f32[384,1024]{1,0:T(8,128)S(1)}, u32[]{:S(2)}, u32[]{:S(2)}) %collective-permute-start.3) | collective-permute-done | bytes 1572896 | tf_op jit(solution)/shard_map/ppermute | solution.py:9
  210.6 0.0 copy-done.1
  210.6 0.9 multiply_reduce_fusion
  211.5 1.5 subtract_divide_fusion
  (6 shorter events, 0.0 us)
Async XLA Ops:
  0.6 21.5 %copy-start = (bf16[384,1024]{1,0:T(8,128)(2,1)S(1)}, bf16[384,1024]{1,0:T(8,128)(2,1)}, u32[]{:S(2)}) copy-start(bf16[384,1024]{1,0:T(8,128)(2,1)} %param.5) | copy-start | bytes 2359300
  3.5 20.6 %copy-start.2 = (s32[384]{0:T(512)S(1)}, s32[384]{0:T(512)}, u32[]{:S(2)}) copy-start(s32[384]{0:T(512)} %param.7) | copy-start | bytes 4612
  3.5 80.3 %collective-permute-start.1 = (bf16[384,1024]{1,0:T(8,128)(2,1)S(1)}, bf16[384,1024]{1,0:T(8,128)(2,1)S(1)}, u32[]{:S(2)}, u32[]{:S(2)}) collective-permute-start(bf16[384,1024]{1,0:T(8,128)(2,1)S(1)} %fusion.35), channel_id=1, source_target_pairs={{0,2},{1,3},{2,4},{3,5},{4,6},{5,7},{6,8},{7,9},{8,10},{9,11},{10,... | collective-permute-start | bytes 2359304 | tf_op jit(solution)/shard_map/ppermute | solution.py:9
  7.8 79.2 %collective-permute-start = (bf16[384,1024]{1,0:T(8,128)(2,1)S(1)}, bf16[384,1024]{1,0:T(8,128)(2,1)S(1)}, u32[]{:S(2)}, u32[]{:S(2)}) collective-permute-start(bf16[384,1024]{1,0:T(8,128)(2,1)S(1)} %fusion.35), channel_id=1, source_target_pairs={{0,1},{1,2},{2,3},{3,4},{4,5},{5,6},{6,7},{7,8},{8,9},{9,10},{10,1... | collective-permute-start | bytes 2359304 | tf_op jit(solution)/shard_map/ppermute | solution.py:9
  18.5 59.5 %collective-permute-start.2 = (bf16[384,1024]{1,0:T(8,128)(2,1)S(1)}, bf16[384,1024]{1,0:T(8,128)(2,1)}, u32[]{:S(2)}, u32[]{:S(2)}) collective-permute-start(bf16[384,1024]{1,0:T(8,128)(2,1)S(1)} %fusion.35), channel_id=1, source_target_pairs={{0,64},{64,128},{128,192},{192,256},{256,320},{320,384},{384,448},... | collective-permute-start | bytes 2359304 | tf_op jit(solution)/shard_map/ppermute | solution.py:9
  80.4 91.8 %collective-permute-start.5 = (f32[384,1024]{1,0:T(8,128)S(1)}, f32[384,1024]{1,0:T(8,128)S(1)}, u32[]{:S(2)}, u32[]{:S(2)}) collective-permute-start(f32[384,1024]{1,0:T(8,128)S(1)} %convolution_multiply_fusion), channel_id=1, source_target_pairs={{0,704},{64,0},{128,64},{192,128},{256,192},{320,256},{384,320},{4... | collective-permute-start | bytes 4718600 | tf_op jit(solution)/shard_map/ppermute | solution.py:9
  85.1 87.0 %collective-permute-start.4 = (f32[384,1024]{1,0:T(8,128)S(1)}, f32[384,1024]{1,0:T(8,128)S(1)}, u32[]{:S(2)}, u32[]{:S(2)}) collective-permute-start(f32[384,1024]{1,0:T(8,128)S(1)} %convolution_multiply_fusion.1), channel_id=1, source_target_pairs={{0,62},{1,63},{2,0},{3,1},{4,2},{5,3},{6,4},{7,5},{8,6},{9,7},{10,... | collective-permute-start | bytes 4718600 | tf_op jit(solution)/shard_map/ppermute | solution.py:9
  88.4 122.2 %collective-permute-start.3 = (f32[384,1024]{1,0:T(8,128)S(1)}, f32[384,1024]{1,0:T(8,128)S(1)}, u32[]{:S(2)}, u32[]{:S(2)}) collective-permute-start(f32[384,1024]{1,0:T(8,128)S(1)} %convolution_multiply_fusion.2), channel_id=1, source_target_pairs={{0,63},{1,0},{2,1},{3,2},{4,3},{5,4},{6,5},{7,6},{8,7},{9,8},{10,9... | collective-permute-start | bytes 4718600 | tf_op jit(solution)/shard_map/ppermute | solution.py:9
  94.1 116.5 %copy-start.1 = (bf16[384,1024]{1,0:T(8,128)(2,1)S(1)}, bf16[384,1024]{1,0:T(8,128)(2,1)}, u32[]{:S(2)}) copy-start(bf16[384,1024]{1,0:T(8,128)(2,1)} %param.6) | copy-start | bytes 2359300
where the time goes:
time: 213 us
  waiting for transfers between devices  168 us (79%)
  starting transfers between devices  25.9 us (12%)
  matrix products  10.4 us (5%)
  other arithmetic  6.33 us (3%)
  between operations  2.28 us (1%)
    ppermute x6, waiting for transfers between devices, from_behind(): lax.ppermute(array, axis, [(i, (i + by) % count) for i in range(count)])  168 us
    ppermute x6, starting transfers between devices, from_behind(): lax.ppermute(array, axis, [(i, (i + by) % count) for i in range(count)])  25.9 us
  transfers between devices with their start and end apart: 6, of which 3 were waited for; matrix products, arithmetic and copies ran while one was open for 5% of the time, Pallas kernels for 0%

commit v1 on v0

v1 whole, which is shorter than its diff:
```python
import jax
import jax.numpy as jnp
from jax import lax
from jax.sharding import PartitionSpec as P

CODE_ROWS = 16
NO_MATCH = -256.0


def from_behind(array, axis, by):
    count = lax.axis_size(axis)
    return lax.ppermute(array, axis, [(i, (i + by) % count) for i in range(count)])


def normalize(values):
    wide = values.astype(jnp.float32)
    norms = jnp.sqrt(jnp.sum(wide * wide, axis=-1, keepdims=True) + 1e-06)
    return (wide / norms, norms)


def rounded(values):
    return normalize(values)[0].astype(jnp.bfloat16)


def back_through(unit, norms, grad):
    return (grad - unit * jnp.sum(unit * grad, axis=-1, keepdims=True)) / norms


def scores_of(rows, columns, multiplier, bias):
    return (
        multiplier
        * lax.dot_general(
            rows, columns, (((1,), (1,)), ((), ())), preferred_element_type=jnp.float32
        )
        + bias
    )


def signal_of(scores, matches):
    labels = jnp.where(matches, 1.0, -1.0).astype(jnp.float32)
    return (-labels * jax.nn.sigmoid(-labels * scores)).astype(jnp.bfloat16)


def dot(a, b):
    return jnp.dot(a, b, preferred_element_type=jnp.float32)


def per_device(image_embed, text_embed, partner, exponent_of_multiplier, logit_bias):
    multiplier = jnp.exp(exponent_of_multiplier[0])
    bias = logit_bias[0]
    cycle = lax.axis_size("blk")
    groups = lax.axis_size("group")
    rows, width = image_embed.shape
    g = lax.axis_index("group")
    b = lax.axis_index("blk")

    def first_of(group_at, cycle_at):
        return (group_at * cycle + cycle_at) * rows

    links = [
        ("blk", 1, first_of(g, (b + cycle - 1) % cycle)),
        ("group", 1, first_of((g + groups - 1) % groups, b)),
        ("blk", 2, first_of(g, (b + cycle - 2) % cycle)),
    ]
    text_in = [from_behind(text_embed, axis, by) for axis, by, _ in links]
    near_image = from_behind(image_embed, "blk", -1)
    near_partner = from_behind(partner, "blk", -1)

    image_unit, image_norm = normalize(image_embed)
    image_round = image_unit.astype(jnp.bfloat16)

    def code_of(partners, text_first):
        place = partners - text_first
        inside = (place >= 0) & (place < rows)
        return jnp.where(inside, (place - rows // 2).astype(jnp.float32), NO_MATCH)

    codes = jnp.stack([code_of(partner, first) for _, _, first in links])
    codes = jnp.pad(codes, ((0, CODE_ROWS - len(links)), (0, width - rows)))
    packed = jnp.concatenate([image_round, codes.astype(jnp.bfloat16)])
    packed, text_in[1], text_in[2] = lax.optimization_barrier((packed, text_in[1], text_in[2]))
    packed_in = [None] + [from_behind(packed, axis, -by) for axis, by, _ in links[1:]]

    text_unit, text_norm = normalize(text_embed)
    text_round = text_unit.astype(jnp.bfloat16)

    columns = jnp.arange(rows, dtype=jnp.int32)

    def forward(text, text_first):
        matches = partner[:, None] == (text_first + columns)[None, :]
        return signal_of(scores_of(image_round, text, multiplier, bias), matches)

    def backward(image, code):
        matches = code[None, :] == (columns - rows // 2).astype(jnp.float32)[:, None]
        return signal_of(scores_of(text_round, image, multiplier, bias), matches)

    own = forward(text_round, first_of(g, b))
    image_sum = dot(own, text_round)
    text_sum = lax.dot_general(
        own, image_round, (((0,), (0,)), ((), ())), preferred_element_type=jnp.float32
    )
    for i in (2, 1, 0):
        text = rounded(text_in[i])
        image_sum = image_sum + dot(forward(text, links[i][2]), text)
        if i > 0:
            image = packed_in[i][:rows]
            code = packed_in[i][rows + i, :rows].astype(jnp.float32)
        else:
            image = rounded(near_image)
            code = code_of(near_partner, first_of(g, b))
        text_sum = text_sum + dot(backward(image, code), image)
    image_grad = back_through(image_unit, image_norm, multiplier * image_sum)
    text_grad = back_through(text_unit, text_norm, multiplier * text_sum)
    return (image_grad, text_grad)


def solution(mesh):
    return jax.shard_map(
        per_device,
        mesh=mesh,
        in_specs=(
            P(("group", "blk"), None),
            P(("group", "blk"), None),
            P(("group", "blk")),
            P(),
            P(),
        ),
        out_specs=(P(("group", "blk"), None), P(("group", "blk"), None)),
        check_vma=False,
    )
```

time: 213 us -> 158 us (0.74)
  the two profiles are of different devices: /device:TPU:287 before, /device:TPU:257 now
where the time goes in v1:
time: 158 us
  waiting for transfers between devices  68.6 us (43%)
  starting transfers between devices  44.1 us (28%)
  matrix products  29.1 us (18%)
  other arithmetic  13.5 us (9%)
  between operations  2.28 us (1%)
    ppermute x7, waiting for transfers between devices, from_behind(): lax.ppermute(array, axis, [(i, (i + by) % count) for i in range(count)])  68.6 us
    ppermute x7, starting transfers between devices, from_behind(): lax.ppermute(array, axis, [(i, (i + by) % count) for i in range(count)])  44.1 us
    dot_general x7, matrix products, dot(): return jnp.dot(a, b, preferred_element_type=jnp.float32)  26.5 us
    reduce_sum x5, other arithmetic, normalize(): norms = jnp.sqrt(jnp.sum(wide * wide, axis=-1, keepdims=True) + 1e-06)  7.29 us
    div x2, other arithmetic, back_through(): return (grad - unit * jnp.sum(unit * grad, axis=-1, keepdims=True)) / norms  4.39 us
  transfers between devices with their start and end apart: 7, of which 1 were waited for; matrix products, arithmetic and copies ran while one was open for 18% of the time, Pallas kernels for 0%

profile of v1, /device:TPU:257, one launch (start us, length us, event | category | flops | bytes accessed | tf_op | source)
XLA Modules:
  0.0 157.6 jit_solution(4662637719890315167)
XLA Ops:
  0.6 0.0 copy-start.2
  0.6 0.0 copy-start
  0.6 4.7 %collective-permute-start = (bf16[384,1024]{1,0:T(8,128)(2,1)}, bf16[384,1024]{1,0:T(8,128)(2,1)}, u32[]{:S(2)}, u32[]{:S(2)}) collective-permute-start(bf16[384,1024]{1,0:T(8,128)(2,1)} %param.6), channel_id=1, source_target_pairs={{0,64},{64,128},{128,192},{192,256},{256,320},{320,384},{384,448},... | collective-permute-start | bytes 2359304 | tf_op jit(solution)/shard_map/ppermute | solution.py:12
  5.4 3.1 %collective-permute-start.1 = (bf16[384,1024]{1,0:T(8,128)(2,1)}, bf16[384,1024]{1,0:T(8,128)(2,1)}, u32[]{:S(2)}, u32[]{:S(2)}) collective-permute-start(bf16[384,1024]{1,0:T(8,128)(2,1)} %param.6), channel_id=1, source_target_pairs={{0,2},{1,3},{2,4},{3,5},{4,6},{5,7},{6,8},{7,9},{8,10},{9,11},{10,... | collective-permute-start | bytes 2359304 | tf_op jit(solution)/shard_map/ppermute | solution.py:12
  8.5 9.8 %collective-permute-start.2 = (bf16[384,1024]{1,0:T(8,128)(2,1)}, bf16[384,1024]{1,0:T(8,128)(2,1)}, u32[]{:S(2)}, u32[]{:S(2)}) collective-permute-start(bf16[384,1024]{1,0:T(8,128)(2,1)} %param.6), channel_id=1, source_target_pairs={{0,1},{1,2},{2,3},{3,4},{4,5},{5,6},{6,7},{7,8},{8,9},{9,10},{10,1... | collective-permute-start | bytes 2359304 | tf_op jit(solution)/shard_map/ppermute | solution.py:12
  18.3 6.1 %collective-permute-start.5 = (s32[384]{0:T(512)}, s32[384]{0:T(512)S(1)}, u32[]{:S(2)}, u32[]{:S(2)}) collective-permute-start(s32[384]{0:T(512)} %param.7), channel_id=1, source_target_pairs={{0,63},{1,0},{2,1},{3,2},{4,3},{5,4},{6,5},{7,6},{8,7},{9,8},{10,9... | collective-permute-start | bytes 4616 | tf_op jit(solution)/shard_map/ppermute | solution.py:12
  24.3 9.4 %collective-permute-start.6 = (bf16[384,1024]{1,0:T(8,128)(2,1)}, bf16[384,1024]{1,0:T(8,128)(2,1)}, u32[]{:S(2)}, u32[]{:S(2)}) collective-permute-start(bf16[384,1024]{1,0:T(8,128)(2,1)} %param.5), channel_id=1, source_target_pairs={{0,63},{1,0},{2,1},{3,2},{4,3},{5,4},{6,5},{7,6},{8,7},{9,8},{10,9... | collective-permute-start | bytes 2359304 | tf_op jit(solution)/shard_map/ppermute | solution.py:12
  33.8 0.0 copy-start.1
  33.8 1.4 fusion
  35.3 1.4 fusion.1
  36.7 0.0 copy-done.2
  36.7 0.0 copy-done
  36.8 0.3 fusion.168
  38.4 0.0 copy-done.1
  38.4 0.8 fusion.65
  39.2 1.8 %fusion.185 = f32[384,1024]{1,0:T(8,128)} fusion(bf16[384,384]{1,0:T(8,128)(2,1)S(1)} %fusion.65, bf16[384,1024]{1,0:T(8,128)(2,1)S(1)} %fusion.168), kind=kOutput, calls=%fused_computation.202 | convolution fusion | flops 301989888 | bytes 2654208 | tf_op jit(solution)/shard_map/dot_general | solution.py:98
  41.0 0.1 pad_maximum_fusion
  41.1 1.8 %fusion.176 = f32[384,1024]{1,0:T(8,128)} fusion(bf16[384,384]{1,0:T(8,128)(2,1)S(1)} %fusion.65, f32[384]{0:T(512)S(1)} %add_sqrt_fusion.4, bf16[384,1024]{1,0:T(8,128)(2,1)S(1)} %copy-done.1), kind=kOutput, calls=%fused_computation.201 | convolution fusion | flops 303169536 | bytes 2655744 | tf_op jit(solution)/shard_map/dot_general | solution.py:45
  42.9 68.6 %collective-permute-done.5 = s32[384]{0:T(512)S(1)} collective-permute-done((s32[384]{0:T(512)}, s32[384]{0:T(512)S(1)}, u32[]{:S(2)}, u32[]{:S(2)}) %collective-permute-start.5) | collective-permute-done | bytes 1568 | tf_op jit(solution)/shard_map/ppermute | solution.py:12
  111.5 0.0 collective-permute-done
  111.5 0.0 collective-permute-done.1
  111.5 9.1 %collective-permute-start.3 = (bf16[400,1024]{1,0:T(8,128)(2,1)S(1)}, bf16[400,1024]{1,0:T(8,128)(2,1)}, u32[]{:S(2)}, u32[]{:S(2)}) collective-permute-start(bf16[400,1024]{1,0:T(8,128)(2,1)S(1)} %pad_maximum_fusion), channel_id=1, source_target_pairs={{0,62},{1,63},{2,0},{3,1},{4,2},{5,3},{6,4},{7,5},{8,6},{9,7},{10,... | collective-permute-start | bytes 2457608 | tf_op jit(solution)/shard_map/ppermute | solution.py:12
  120.6 1.9 %collective-permute-start.4 = (bf16[400,1024]{1,0:T(8,128)(2,1)S(1)}, bf16[400,1024]{1,0:T(8,128)(2,1)}, u32[]{:S(2)}, u32[]{:S(2)}) collective-permute-start(bf16[400,1024]{1,0:T(8,128)(2,1)S(1)} %pad_maximum_fusion), channel_id=1, source_target_pairs={{0,704},{64,0},{128,64},{192,128},{256,192},{320,256},{384,320},{4... | collective-permute-start | bytes 2457608 | tf_op jit(solution)/shard_map/ppermute | solution.py:12
  122.5 1.8 %fusion.2 = (f32[384]{0:T(512)S(1)}, f32[384]{0:T(512)S(1)}) fusion(bf16[384,1024]{1,0:T(8,128)(2,1)} %collective-permute-done.1, bf16[384,1024]{1,0:T(8,128)(2,1)} %collective-permute-done), kind=kLoop, calls=%fused_computation.14 | loop fusion | flops 2358528 | bytes 1575936 | tf_op jit(solution)/shard_map/reduce_sum | solution.py:17
  124.3 0.0 collective-permute-done.2
  124.3 1.4 fusion.6
  125.7 3.8 %fusion.66 = f32[384,1024]{1,0:T(8,128)} fusion(bf16[384,1024]{1,0:T(8,128)(2,1)S(1)} %fusion.168, bf16[384,1024]{1,0:T(8,128)(2,1)} %collective-permute-done.1, f32[384]{0:T(512)S(1)} %add_sqrt_fusion.3, s32[384]{0:T(512)S(1)} %iota_add_fusion.2, f32[]{:T(128)} %bitcast.15, f32[]{:T(128)} %bitcast, s32[384]{0:T(512)S(1)} %copy-done.2), kind=kOutput, calls=%fused_computation.91 | convolution fusion | flops 607961088 | bytes 3150344 | tf_op jit(solution)/shard_map/dot_general | solution.py:45
  129.5 3.8 %fusion.67 = f32[384,1024]{1,0:T(8,128)} fusion(bf16[384,1024]{1,0:T(8,128)(2,1)S(1)} %fusion.168, bf16[384,1024]{1,0:T(8,128)(2,1)} %collective-permute-done, f32[384]{0:T(512)S(1)} %add_sqrt_fusion.2, s32[384]{0:T(512)S(1)} %iota_add_fusion.1, f32[]{:T(128)} %bitcast.14, f32[]{:T(128)} %bitcast, s32[384]{0:T(512)S(1)} %copy-done.2), kind=kOutput, calls=%fused_computation.92 | convolution fusion | flops 607961088 | bytes 3150344 | tf_op jit(solution)/shard_map/dot_general | solution.py:45
  133.3 5.4 %multiply_reduce_fusion.1 = (f32[384]{0:T(512)S(1)}, f32[384,1024]{1,0:T(8,128)}) fusion(f32[384]{0:T(512)S(1)} %add_sqrt_fusion.5, bf16[384,1024]{1,0:T(8,128)(2,1)S(1)} %copy-done, bf16[384,1024]{1,0:T(8,128)(2,1)} %collective-permute-done.2, f32[384]{0:T(512)S(1)} %add_sqrt_fusion.1, bf16[384,1024]{1,0:T(8,128)(2,1)S(1)} %fusion.168, ...), kind=kOutput, calls=%fused_computation.26 | convolution fusion | flops 611106432 | bytes 8658440 | tf_op jit(solution)/shard_map/dot_general | solution.py:45
  138.7 0.0 collective-permute-done.6
  138.7 1.4 fusion.8
  140.0 2.9 %subtract_divide_fusion.1 = f32[384,1024]{1,0:T(8,128)} fusion(f32[384,1024]{1,0:T(8,128)} %get-tuple-element.12, f32[384]{0:T(512)S(1)} %get-tuple-element.11, f32[384]{0:T(512)S(1)} %add_sqrt_fusion.5, bf16[384,1024]{1,0:T(8,128)(2,1)S(1)} %copy-done), kind=kLoop, calls=%fused_computation.25 | loop fusion | flops 1966080 | bytes 3935232 | tf_op jit(solution)/shard_map/div | solution.py:26
  142.9 0.0 collective-permute-done.3
  142.9 0.7 fusion.155
  143.7 0.0 collective-permute-done.4
  143.7 0.7 fusion.154
  144.4 3.7 %fusion.68 = f32[384,1024]{1,0:T(8,128)} fusion(bf16[400,1024]{1,0:T(8,128)(2,1)} %collective-permute-done.3, f32[384]{0:T(512)S(1)} %fusion.155, f32[]{:T(128)} %bitcast.12, f32[]{:T(128)} %bitcast, f32[384]{0:T(512)S(1)} %add_convert_fusion, f32[384]{0:T(512)S(1)} %add_sqrt_fusion.4, bf16[384,1024]{1,0:T(8,128)(2,1)S(1)} %copy-done.1), kind=kOutput, calls=%fused_computation.93 | convolution fusion | flops 606781440 | bytes 3937792 | tf_op jit(solution)/shard_map/dot_general | solution.py:45
  148.1 3.7 %fusion.69 = f32[384,1024]{1,0:T(8,128)} fusion(bf16[400,1024]{1,0:T(8,128)(2,1)} %collective-permute-done.4, f32[384]{0:T(512)S(1)} %fusion.154, f32[]{:T(128)} %bitcast.11, f32[]{:T(128)} %bitcast, f32[384]{0:T(512)S(1)} %add_convert_fusion, f32[384]{0:T(512)S(1)} %add_sqrt_fusion.4, bf16[384,1024]{1,0:T(8,128)(2,1)S(1)} %copy-done.1), kind=kOutput, calls=%fused_computation.94 | convolution fusion | flops 606781440 | bytes 3937792 | tf_op jit(solution)/shard_map/dot_general | solution.py:45
  151.8 4.3 %multiply_reduce_fusion = (f32[384]{0:T(512)S(1)}, f32[384,1024]{1,0:T(8,128)S(1)}) fusion(f32[384]{0:T(512)S(1)} %add_sqrt_fusion.4, bf16[384,1024]{1,0:T(8,128)(2,1)S(1)} %copy-done.1, bf16[384,1024]{1,0:T(8,128)(2,1)} %collective-permute-done.6, f32[384]{0:T(512)S(1)} %add_sqrt_fusion, f32[384]{0:T(512)S(1)} %convert_select_fusion, f32[]{:T(128)} %bitcast.10, ...), kind=kOutput, calls=%fused_computation.23 | convolution fusion | flops 612286080 | bytes 7872008 | tf_op jit(solution)/shard_map/dot_general | solution.py:45
  156.1 1.5 subtract_divide_fusion
  (17 shorter events, 0.1 us)
Async XLA Ops:
  0.6 36.0 %copy-start.2 = (s32[384]{0:T(512)S(1)}, s32[384]{0:T(512)}, u32[]{:S(2)}) copy-start(s32[384]{0:T(512)} %param.7) | copy-start | bytes 4612
  0.6 36.1 %copy-start = (bf16[384,1024]{1,0:T(8,128)(2,1)S(1)}, bf16[384,1024]{1,0:T(8,128)(2,1)}, u32[]{:S(2)}) copy-start(bf16[384,1024]{1,0:T(8,128)(2,1)} %param.5) | copy-start | bytes 2359300
  0.6 110.8 %collective-permute-start = (bf16[384,1024]{1,0:T(8,128)(2,1)}, bf16[384,1024]{1,0:T(8,128)(2,1)}, u32[]{:S(2)}, u32[]{:S(2)}) collective-permute-start(bf16[384,1024]{1,0:T(8,128)(2,1)} %param.6), channel_id=1, source_target_pairs={{0,64},{64,128},{128,192},{192,256},{256,320},{320,384},{384,448},... | collective-permute-start | bytes 2359304 | tf_op jit(solution)/shard_map/ppermute | solution.py:12
  5.4 106.1 %collective-permute-start.1 = (bf16[384,1024]{1,0:T(8,128)(2,1)}, bf16[384,1024]{1,0:T(8,128)(2,1)}, u32[]{:S(2)}, u32[]{:S(2)}) collective-permute-start(bf16[384,1024]{1,0:T(8,128)(2,1)} %param.6), channel_id=1, source_target_pairs={{0,2},{1,3},{2,4},{3,5},{4,6},{5,7},{6,8},{7,9},{8,10},{9,11},{10,... | collective-permute-start | bytes 2359304 | tf_op jit(solution)/shard_map/ppermute | solution.py:12
  8.5 115.8 %collective-permute-start.2 = (bf16[384,1024]{1,0:T(8,128)(2,1)}, bf16[384,1024]{1,0:T(8,128)(2,1)}, u32[]{:S(2)}, u32[]{:S(2)}) collective-permute-start(bf16[384,1024]{1,0:T(8,128)(2,1)} %param.6), channel_id=1, source_target_pairs={{0,1},{1,2},{2,3},{3,4},{4,5},{5,6},{6,7},{7,8},{8,9},{9,10},{10,1... | collective-permute-start | bytes 2359304 | tf_op jit(solution)/shard_map/ppermute | solution.py:12
  18.3 93.2 %collective-permute-start.5 = (s32[384]{0:T(512)}, s32[384]{0:T(512)S(1)}, u32[]{:S(2)}, u32[]{:S(2)}) collective-permute-start(s32[384]{0:T(512)} %param.7), channel_id=1, source_target_pairs={{0,63},{1,0},{2,1},{3,2},{4,3},{5,4},{6,5},{7,6},{8,7},{9,8},{10,9... | collective-permute-start | bytes 4616 | tf_op jit(solution)/shard_map/ppermute | solution.py:12
  24.3 114.3 %collective-permute-start.6 = (bf16[384,1024]{1,0:T(8,128)(2,1)}, bf16[384,1024]{1,0:T(8,128)(2,1)}, u32[]{:S(2)}, u32[]{:S(2)}) collective-permute-start(bf16[384,1024]{1,0:T(8,128)(2,1)} %param.5), channel_id=1, source_target_pairs={{0,63},{1,0},{2,1},{3,2},{4,3},{5,4},{6,5},{7,6},{8,7},{9,8},{10,9... | collective-permute-start | bytes 2359304 | tf_op jit(solution)/shard_map/ppermute | solution.py:12
  33.8 4.6 %copy-start.1 = (bf16[384,1024]{1,0:T(8,128)(2,1)S(1)}, bf16[384,1024]{1,0:T(8,128)(2,1)}, u32[]{:S(2)}) copy-start(bf16[384,1024]{1,0:T(8,128)(2,1)} %param.6) | copy-start | bytes 2359300
  111.5 31.5 %collective-permute-start.3 = (bf16[400,1024]{1,0:T(8,128)(2,1)S(1)}, bf16[400,1024]{1,0:T(8,128)(2,1)}, u32[]{:S(2)}, u32[]{:S(2)}) collective-permute-start(bf16[400,1024]{1,0:T(8,128)(2,1)S(1)} %pad_maximum_fusion), channel_id=1, source_target_pairs={{0,62},{1,63},{2,0},{3,1},{4,2},{5,3},{6,4},{7,5},{8,6},{9,7},{10,... | collective-permute-start | bytes 2457608 | tf_op jit(solution)/shard_map/ppermute | solution.py:12
  120.6 23.1 %collective-permute-start.4 = (bf16[400,1024]{1,0:T(8,128)(2,1)S(1)}, bf16[400,1024]{1,0:T(8,128)(2,1)}, u32[]{:S(2)}, u32[]{:S(2)}) collective-permute-start(bf16[400,1024]{1,0:T(8,128)(2,1)S(1)} %pad_maximum_fusion), channel_id=1, source_target_pairs={{0,704},{64,0},{128,64},{192,128},{256,192},{320,256},{384,320},{4... | collective-permute-start | bytes 2457608 | tf_op jit(solution)/shard_map/ppermute | solution.py:12

commit v2 on v1

v2 whole, which is shorter than its diff:
```python
import functools

import jax
import jax.numpy as jnp
from jax import lax
from jax.experimental import pallas as pl
from jax.experimental.pallas import tpu as pltpu
from jax.sharding import PartitionSpec as P

CODE_ROWS = 16
NO_MATCH = -256.0
VMEM_LIMIT = 32 * 1024 * 1024
LAST_ROWS = 128
BLK_1, GROUP_1, BLK_2, OWN = range(4)


def units_of(values):
    wide = values.astype(jnp.float32)
    scale = lax.rsqrt(jnp.sum(wide * wide, axis=-1, keepdims=True) + 1e-06)
    return wide * scale, scale


def write_codes(ints, partner_ref, out_ref):
    rows, width = partner_ref.shape[0], out_ref.shape[1]
    partner = partner_ref[...].reshape(1, rows)
    row = lax.broadcasted_iota(jnp.int32, (CODE_ROWS, rows), 0)
    codes = jnp.full((CODE_ROWS, rows), NO_MATCH, jnp.float32)
    for kind in range(4):
        place = partner - ints[kind]
        inside = (place >= 0) & (place < rows)
        code = jnp.where(inside, (place - rows // 2).astype(jnp.float32), NO_MATCH)
        codes = jnp.where(row == kind, code, codes)
    out_ref[rows:, :rows] = codes.astype(out_ref.dtype)
    out_ref[rows:, rows:] = jnp.zeros((CODE_ROWS, width - rows), out_ref.dtype)


def first_kernel(ints, image_ref, text_ref, partner_ref, out_ref, done):
    rows = image_ref.shape[0]

    def bring(ref):
        copy = pltpu.make_async_copy(ref, out_ref.at[:rows, :], done)
        copy.start()
        copy.wait()

    pl.when(ints[4] != 0)(lambda: bring(image_ref))
    pl.when(ints[4] == 0)(lambda: bring(text_ref))
    write_codes(ints, partner_ref, out_ref)


def second_kernel(ints, image_ref, text_ref, partner_ref, packed_ref, out_ref):
    rows = image_ref.shape[0]
    packed_ref[:rows, :] = units_of(image_ref[...])[0].astype(packed_ref.dtype)
    write_codes(ints, partner_ref, packed_ref)

    @pl.when(ints[4] == 0)
    def _():
        out_ref[...] = packed_ref[...]

    @pl.when(ints[4] != 0)
    def _():
        out_ref[:rows, :] = text_ref[...]
        out_ref[rows:, :] = jnp.zeros((CODE_ROWS, text_ref.shape[1]), out_ref.dtype)


def pack(kernel, outs, ints, image, text, partner, copies=False):
    rows, width = image.shape
    vmem = pl.BlockSpec(memory_space=pltpu.VMEM)
    given = pl.BlockSpec(memory_space=pl.ANY) if copies else vmem
    return pl.pallas_call(
        kernel,
        out_shape=[jax.ShapeDtypeStruct((rows + CODE_ROWS, width), jnp.bfloat16)] * outs,
        in_specs=[pl.BlockSpec(memory_space=pltpu.SMEM), given, given, vmem],
        out_specs=[vmem] * outs,
        scratch_shapes=[pltpu.SemaphoreType.DMA] if copies else [],
        compiler_params=pltpu.CompilerParams(vmem_limit_bytes=VMEM_LIMIT),
        cost_estimate=pl.CostEstimate(
            flops=4 * rows * width, bytes_accessed=4 * rows * width, transcendentals=rows
        ),
    )(ints, image, text, partner)


def term(side, kind, ints, floats, unit, foreign_ref, other, partner_ref):
    rows = unit.shape[0]
    block = foreign_ref[...]
    if other is not None:
        other_ref, taken = other
        block = jnp.where(ints[taken] != 0, other_ref[: block.shape[0], :], block)
    if side == "image":
        foreign = units_of(block[:rows, :])[0].astype(jnp.bfloat16)
    elif other is not None:
        foreign = jnp.where(
            ints[taken] != 0, units_of(block[:rows, :])[0].astype(jnp.bfloat16), block[:rows, :]
        )
    else:
        foreign = block[:rows, :]
    scores = (
        floats[0]
        * lax.dot_general(
            unit.astype(jnp.bfloat16),
            foreign,
            (((1,), (1,)), ((), ())),
            preferred_element_type=jnp.float32,
        )
        + floats[1]
    )
    if side == "image":
        columns = ints[kind] + lax.broadcasted_iota(jnp.int32, scores.shape, 1)
        matches = partner_ref[...] == columns
    else:
        code = block[rows:, :rows].astype(jnp.float32)[kind : kind + 1, :]
        place = lax.broadcasted_iota(jnp.int32, scores.shape, 0) - rows // 2
        matches = place.astype(jnp.float32) == code
    slope = jax.nn.sigmoid(jnp.where(matches, -scores, scores))
    signal = jnp.where(matches, -slope, slope).astype(jnp.bfloat16)
    return jnp.dot(signal, foreign, preferred_element_type=jnp.float32)


def sum_kernel(plan, last, ints, floats, *refs):
    refs = list(refs)
    partner_ref = refs.pop(0)
    copies = []
    if last:
        done = refs.pop()
        held_refs = [refs.pop() for _ in plan]
    out_refs = refs[-len(plan) :]
    for at, ((side, continues, kinds), out_ref) in enumerate(zip(plan, out_refs)):
        own_ref = refs.pop(0)
        unit, scale = units_of(own_ref[...])
        total = refs.pop(0)[...] if continues else None
        for kind, taken in kinds:
            foreign_ref = refs.pop(0)
            other = None if taken is None else (refs.pop(0), taken)
            more = term(side, kind, ints, floats, unit, foreign_ref, other, partner_ref)
            total = more if total is None else total + more
        if not last:
            out_ref[...] = total
            continue
        held = held_refs[at]
        for n, start in enumerate(range(0, total.shape[0], LAST_ROWS)):
            here = slice(start, start + LAST_ROWS)
            part = floats[0] * total[here]
            along = jnp.sum(unit[here] * part, axis=-1, keepdims=True)
            held[here, :] = (part - unit[here] * along) * scale[here]
            copy = pltpu.make_async_copy(held.at[here, :], out_ref.at[here, :], done.at[at, n])
            copy.start()
            copies.append(copy)
    for copy in copies:
        copy.wait()


def sums(ints, floats, partner, own, work, last=False):
    plan, args = [], [partner]
    for side, (so_far, links) in work.items():
        plan.append((side, so_far is not None, tuple((k, i if o is not None else None) for k, _, o, i in links)))
        args.append(own[side])
        if so_far is not None:
            args.append(so_far)
        for _, block, other, _ in links:
            args += [block] if other is None else [block, other]
    rows, width = own["image"].shape
    terms = sum(len(links) for _, links in work.values())
    vmem = pl.BlockSpec(memory_space=pltpu.VMEM)
    return pl.pallas_call(
        functools.partial(sum_kernel, tuple(plan), last),
        out_shape=[jax.ShapeDtypeStruct((rows, width), jnp.float32)] * len(plan),
        in_specs=[pl.BlockSpec(memory_space=pltpu.SMEM)] * 2 + [vmem] * len(args),
        out_specs=[pl.BlockSpec(memory_space=pl.ANY) if last else vmem] * len(plan),
        scratch_shapes=[pltpu.VMEM((rows, width), jnp.float32)] * len(plan)
        + [pltpu.SemaphoreType.DMA((len(plan), rows // LAST_ROWS))]
        if last
        else [],
        compiler_params=pltpu.CompilerParams(vmem_limit_bytes=VMEM_LIMIT),
        cost_estimate=pl.CostEstimate(
            flops=4 * terms * rows * rows * width,
            bytes_accessed=12 * terms * rows * width,
            transcendentals=terms * rows * rows,
        ),
    )(ints, floats, *args)


def per_device(image_embed, text_embed, partner, exponent_of_multiplier, logit_bias):
    floats = jnp.concatenate([jnp.exp(exponent_of_multiplier), logit_bias])
    cycle = lax.axis_size("blk")
    groups = lax.axis_size("group")
    rows = image_embed.shape[0]
    g = lax.axis_index("group")
    b = lax.axis_index("blk")

    def send(array, target):
        pairs = []
        for i in range(groups):
            for j in range(cycle):
                to = target(i, j)
                if to is not None:
                    pairs.append((i * cycle + j, (to[0] % groups) * cycle + to[1] % cycle))
        return lax.ppermute(array, ("group", "blk"), pairs)

    def first_of(group_at, cycle_at):
        return (group_at * cycle + cycle_at) * rows

    text_first = [
        first_of(g, (b + cycle - 1) % cycle),
        first_of((g + groups - 1) % groups, b),
        first_of(g, (b + cycle - 2) % cycle),
        first_of(g, b),
    ]
    ints = jnp.stack(text_first + [jnp.int32(g == 0), jnp.int32(g == groups - 1)])
    is_first, is_last = 4, 5
    partner_column = partner[:, None]

    (early,) = pack(first_kernel, 1, ints, image_embed, text_embed, partner, copies=True)
    early, image_again, text_again = lax.optimization_barrier((early, image_embed, text_embed))
    early_in = send(early, lambda i, j: (i, j - 1) if i == 0 else (i, j + 1))
    packed, late = pack(second_kernel, 2, ints, image_again, text_embed, partner)
    x_text = send(text_again, lambda i, j: (i, j + 2))
    x_image = send(packed, lambda i, j: (i, j - 2))
    late_in = send(late, lambda i, j: (i, j + 1) if i == 0 else (i, j - 1))
    packed, text_again = lax.optimization_barrier((packed, text_again))
    group_text = send(text_again, lambda i, j: (i + 1, j) if i < groups - 1 else None)
    handed = send(
        early_in,
        lambda i, j: (groups - 1, j + 1) if i == 0 else (0, j - 1) if i == groups - 1 else None,
    )
    packed_again, early_in = lax.optimization_barrier((packed, early_in))
    group_image = send(packed_again, lambda i, j: (i - 1, j) if i > 0 else None)

    step = functools.partial(sums, ints, floats, partner_column, {"image": image_embed, "text": text_embed})
    image_sum, text_sum = step({
        "image": (None, [(OWN, text_embed, None, None), (BLK_2, x_text, None, None)]),
        "text": (None, [(OWN, packed, None, None), (BLK_2, x_image, None, None)]),
    })
    image_sum, text_sum = step({
        "image": (image_sum, [(BLK_1, early_in, late_in, is_first)]),
        "text": (text_sum, [(BLK_1, late_in, early_in, is_first)]),
    })
    return step({
        "image": (image_sum, [(GROUP_1, group_text, handed, is_first)]),
        "text": (text_sum, [(GROUP_1, group_image, handed, is_last)]),
    }, last=True)


def solution(mesh):
    return jax.shard_map(
        per_device,
        mesh=mesh,
        in_specs=(
            P(("group", "blk"), None),
            P(("group", "blk"), None),
            P(("group", "blk")),
            P(),
            P(),
        ),
        out_specs=(P(("group", "blk"), None), P(("group", "blk"), None)),
        check_vma=False,
    )
```

time: 158 us -> 142 us (0.90)
  the two profiles are of different devices: /device:TPU:257 before, /device:TPU:1 now
where the time goes in v2:
time: 142 us; the launch traced here: 141 us
  starting transfers between devices  81.7 us (58%)
  waiting for transfers between devices  40.2 us (28%)
  Pallas kernels  14.2 us (10%)
  local copies, waits for them, and re-layouts  3.14 us (2%)
  between operations  2.13 us (2%)
    ppermute x7, starting transfers between devices, send(): return lax.ppermute(array, ('group', 'blk'), pairs)  81.7 us
    ppermute x7, waiting for transfers between devices, send(): return lax.ppermute(array, ('group', 'blk'), pairs)  40.2 us
    pallas_call x3, Pallas kernels, sums(): pl.pallas_call(functools.partial(sum_kernel, tuple(plan), last), out_shap...  12.7 us
    unnamed x6, local copies, waits for them, and re-layouts  2.95 us
  transfers between devices with their start and end apart: 7, of which 4 were waited for; matrix products, arithmetic and copies ran while one was open for 0% of the time, Pallas kernels for 6%

profile of v2, /device:TPU:1, one launch (start us, length us, event | category | flops | bytes accessed | tf_op | source)
XLA Modules:
  0.0 141.4 jit_solution(5222832243689330893)
XLA Ops:
  0.7 0.1 stack.35.ints
  0.8 0.0 copy-start
  0.8 1.1 copy-done
  1.9 0.0 copy-start.1
  1.9 1.1 copy-done.1
  3.0 0.0 copy-start.2
  3.0 0.7 copy-done.2
  3.7 0.6 shard_map.68
  4.4 15.7 %collective-permute-start.2 = (bf16[400,1024]{1,0:T(8,128)(2,1)S(1)}, bf16[400,1024]{1,0:T(8,128)(2,1)S(1)}, u32[]{:S(2)}, u32[]{:S(2)}) collective-permute-start(bf16[400,1024]{1,0:T(8,128)(2,1)S(1)} %shard_map.68), channel_id=1, source_target_pairs={{0,63},{1,0},{2,1},{3,2},{4,3},{5,4},{6,5},{7,6},{8,7},{9,8},{10,9... | collective-permute-start | bytes 2457608 | tf_op jit(solution)/shard_map/ppermute | solution.py:196
  20.1 3.1 %collective-permute-start = (bf16[384,1024]{1,0:T(8,128)(2,1)S(1)}, bf16[384,1024]{1,0:T(8,128)(2,1)S(1)}, u32[]{:S(2)}, u32[]{:S(2)}) collective-permute-start(bf16[384,1024]{1,0:T(8,128)(2,1)S(1)} %copy-done.1), channel_id=1, source_target_pairs={{0,2},{1,3},{2,4},{3,5},{4,6},{5,7},{6,8},{7,9},{8,10},{9,11},{10,... | collective-permute-start | bytes 2359304 | tf_op jit(solution)/shard_map/ppermute | solution.py:196
  23.2 0.9 shard_map.69
  24.0 6.1 %collective-permute-start.1 = (bf16[400,1024]{1,0:T(8,128)(2,1)S(1)}, bf16[400,1024]{1,0:T(8,128)(2,1)S(1)}, u32[]{:S(2)}, u32[]{:S(2)}) collective-permute-start(bf16[400,1024]{1,0:T(8,128)(2,1)S(1)} %get-tuple-element.27.refs_5_), channel_id=1, source_target_pairs={{0,62},{1,63},{2,0},{3,1},{4,2},{5,3},{6,4},{7,5},{8,6},{9,7},{10,... | collective-permute-start | bytes 2457608 | tf_op jit(solution)/shard_map/ppermute | solution.py:196
  30.1 3.1 %collective-permute-start.3 = (bf16[400,1024]{1,0:T(8,128)(2,1)S(1)}, bf16[400,1024]{1,0:T(8,128)(2,1)S(1)}, u32[]{:S(2)}, u32[]{:S(2)}) collective-permute-start(bf16[400,1024]{1,0:T(8,128)(2,1)S(1)} %get-tuple-element.22), channel_id=1, source_target_pairs={{0,1},{1,2},{2,3},{3,4},{4,5},{5,6},{6,7},{7,8},{8,9},{9,10},{10,1... | collective-permute-start | bytes 2457608 | tf_op jit(solution)/shard_map/ppermute | solution.py:196
  33.2 11.3 %collective-permute-done.2.refs_3_.refs_8_ = bf16[400,1024]{1,0:T(8,128)(2,1)S(1)} collective-permute-done((bf16[400,1024]{1,0:T(8,128)(2,1)S(1)}, bf16[400,1024]{1,0:T(8,128)(2,1)S(1)}, u32[]{:S(2)}, u32[]{:S(2)}) %collective-permute-start.2) | collective-permute-done | bytes 819232 | tf_op jit(solution)/shard_map/ppermute | solution.py:196
  44.5 4.0 %collective-permute-start.6 = (bf16[400,1024]{1,0:T(8,128)(2,1)S(1)}, bf16[400,1024]{1,0:T(8,128)(2,1)S(1)}, u32[]{:S(2)}, u32[]{:S(2)}) collective-permute-start(bf16[400,1024]{1,0:T(8,128)(2,1)S(1)} %get-tuple-element.27.refs_5_), channel_id=1, source_target_pairs={{64,0},{65,1},{66,2},{67,3},{68,4},{69,5},{70,6},{71,7},{72,8},{73... | collective-permute-start | bytes 2457608 | tf_op jit(solution)/shard_map/ppermute | solution.py:196
  48.5 0.7 collective-permute-start.5
  49.2 0.2 collective-permute-done.refs_3_
  49.4 49.0 %collective-permute-start.4 = (bf16[384,1024]{1,0:T(8,128)(2,1)S(1)}, bf16[384,1024]{1,0:T(8,128)(2,1)S(1)}, u32[]{:S(2)}, u32[]{:S(2)}) collective-permute-start(bf16[384,1024]{1,0:T(8,128)(2,1)S(1)} %copy-done.1), channel_id=1, source_target_pairs={{0,64},{1,65},{2,66},{3,67},{4,68},{5,69},{6,70},{7,71},{8,72},{9,... | collective-permute-start | bytes 2359304 | tf_op jit(solution)/shard_map/ppermute | solution.py:196
  98.4 0.1 broadcast_in_dim.4.refs_0_
  99.9 0.1 pad_maximum_fusion.floats
  100.0 0.0 collective-permute-done.1.refs_6_
  100.0 4.5 %shard_map.70 = (f32[384,1024]{1,0:T(8,128)S(1)}, f32[384,1024]{1,0:T(8,128)S(1)}) custom-call(s32[6]{0:T(128)S(1)} %stack.35.ints, f32[2]{0:T(128)S(1)} %pad_maximum_fusion.floats, s32[384,1]{1,0:T(8,128)S(1)} %broadcast_in_dim.4.refs_0_, bf16[384,1024]{1,0:T(8,128)(2,1)S(1)} %copy-done, bf16[384,1024]{1,0:T(8,128)(2,1)S(1)} %copy-done.1, ...), custom_call_target="tpu_custom_call" | custom-call | flops 2415919104 | bytes 18874368 | tf_op jit(solution)/shard_map/pallas_call | solution.py:163
  104.5 0.0 collective-permute-done.3.refs_4_.refs_7_
  104.5 3.3 %shard_map.71 = (f32[384,1024]{1,0:T(8,128)S(1)}, f32[384,1024]{1,0:T(8,128)S(1)}) custom-call(s32[6]{0:T(128)S(1)} %stack.35.ints, f32[2]{0:T(128)S(1)} %pad_maximum_fusion.floats, s32[384,1]{1,0:T(8,128)S(1)} %broadcast_in_dim.4.refs_0_, bf16[384,1024]{1,0:T(8,128)(2,1)S(1)} %copy-done, f32[384,1024]{1,0:T(8,128)S(1)} %get-tuple-element.19.refs_2_, ...), custom_call_target="tpu_custom_call" | custom-call | flops 1207959552 | bytes 9437184 | tf_op jit(solution)/shard_map/pallas_call | solution.py:163
  107.8 26.1 %collective-permute-done.4.refs_3_ = bf16[384,1024]{1,0:T(8,128)(2,1)S(1)} collective-permute-done((bf16[384,1024]{1,0:T(8,128)(2,1)S(1)}, bf16[384,1024]{1,0:T(8,128)(2,1)S(1)}, u32[]{:S(2)}, u32[]{:S(2)}) %collective-permute-start.4) | collective-permute-done | bytes 786464 | tf_op jit(solution)/shard_map/ppermute | solution.py:196
  133.9 2.6 %collective-permute-done.6.refs_7_ = bf16[400,1024]{1,0:T(8,128)(2,1)S(1)} collective-permute-done((bf16[400,1024]{1,0:T(8,128)(2,1)S(1)}, bf16[400,1024]{1,0:T(8,128)(2,1)S(1)}, u32[]{:S(2)}, u32[]{:S(2)}) %collective-permute-start.6) | collective-permute-done | bytes 819232 | tf_op jit(solution)/shard_map/ppermute | solution.py:196
  136.5 0.0 collective-permute-done.5.refs_4_.refs_8_
  136.5 4.9 %shard_map.72 = (f32[384,1024]{1,0:T(8,128)}, f32[384,1024]{1,0:T(8,128)}) custom-call(s32[6]{0:T(128)S(1)} %stack.35.ints, f32[2]{0:T(128)S(1)} %pad_maximum_fusion.floats, s32[384,1]{1,0:T(8,128)S(1)} %broadcast_in_dim.4.refs_0_, bf16[384,1024]{1,0:T(8,128)(2,1)S(1)} %copy-done, f32[384,1024]{1,0:T(8,128)S(1)} %get-tuple-element.24.refs_2_, ...), custom_call_target="tpu_custom_call" | custom-call | flops 1207959552 | bytes 9437184 | tf_op jit(solution)/shard_map/pallas_call | solution.py:163
Async XLA Ops:
  0.8 1.1 copy-start
  1.9 1.1 copy-start.1
  3.0 0.7 copy-start.2
  4.4 40.2 %collective-permute-start.2 = (bf16[400,1024]{1,0:T(8,128)(2,1)S(1)}, bf16[400,1024]{1,0:T(8,128)(2,1)S(1)}, u32[]{:S(2)}, u32[]{:S(2)}) collective-permute-start(bf16[400,1024]{1,0:T(8,128)(2,1)S(1)} %shard_map.68), channel_id=1, source_target_pairs={{0,63},{1,0},{2,1},{3,2},{4,3},{5,4},{6,5},{7,6},{8,7},{9,8},{10,9... | collective-permute-start | bytes 2457608 | tf_op jit(solution)/shard_map/ppermute | solution.py:196
  20.1 29.4 %collective-permute-start = (bf16[384,1024]{1,0:T(8,128)(2,1)S(1)}, bf16[384,1024]{1,0:T(8,128)(2,1)S(1)}, u32[]{:S(2)}, u32[]{:S(2)}) collective-permute-start(bf16[384,1024]{1,0:T(8,128)(2,1)S(1)} %copy-done.1), channel_id=1, source_target_pairs={{0,2},{1,3},{2,4},{3,5},{4,6},{5,7},{6,8},{7,9},{8,10},{9,11},{10,... | collective-permute-start | bytes 2359304 | tf_op jit(solution)/shard_map/ppermute | solution.py:196
  24.0 75.9 %collective-permute-start.1 = (bf16[400,1024]{1,0:T(8,128)(2,1)S(1)}, bf16[400,1024]{1,0:T(8,128)(2,1)S(1)}, u32[]{:S(2)}, u32[]{:S(2)}) collective-permute-start(bf16[400,1024]{1,0:T(8,128)(2,1)S(1)} %get-tuple-element.27.refs_5_), channel_id=1, source_target_pairs={{0,62},{1,63},{2,0},{3,1},{4,2},{5,3},{6,4},{7,5},{8,6},{9,7},{10,... | collective-permute-start | bytes 2457608 | tf_op jit(solution)/shard_map/ppermute | solution.py:196
  30.1 74.4 %collective-permute-start.3 = (bf16[400,1024]{1,0:T(8,128)(2,1)S(1)}, bf16[400,1024]{1,0:T(8,128)(2,1)S(1)}, u32[]{:S(2)}, u32[]{:S(2)}) collective-permute-start(bf16[400,1024]{1,0:T(8,128)(2,1)S(1)} %get-tuple-element.22), channel_id=1, source_target_pairs={{0,1},{1,2},{2,3},{3,4},{4,5},{5,6},{6,7},{7,8},{8,9},{9,10},{10,1... | collective-permute-start | bytes 2457608 | tf_op jit(solution)/shard_map/ppermute | solution.py:196
  44.5 92.0 %collective-permute-start.6 = (bf16[400,1024]{1,0:T(8,128)(2,1)S(1)}, bf16[400,1024]{1,0:T(8,128)(2,1)S(1)}, u32[]{:S(2)}, u32[]{:S(2)}) collective-permute-start(bf16[400,1024]{1,0:T(8,128)(2,1)S(1)} %get-tuple-element.27.refs_5_), channel_id=1, source_target_pairs={{64,0},{65,1},{66,2},{67,3},{68,4},{69,5},{70,6},{71,7},{72,8},{73... | collective-permute-start | bytes 2457608 | tf_op jit(solution)/shard_map/ppermute | solution.py:196
  48.5 88.0 %collective-permute-start.5 = (bf16[400,1024]{1,0:T(8,128)(2,1)S(1)}, bf16[400,1024]{1,0:T(8,128)(2,1)S(1)}, u32[]{:S(2)}, u32[]{:S(2)}) collective-permute-start(bf16[400,1024]{1,0:T(8,128)(2,1)S(1)} %collective-permute-done.2.refs_3_.refs_8_), channel_id=1, source_target_pairs={{0,705},{1,706},{2,707},{3,708},{4,709},{5,710},{6,711},{7,712},{8... | collective-permute-start | bytes 2457608 | tf_op jit(solution)/shard_map/ppermute | solution.py:196
  49.4 84.5 %collective-permute-start.4 = (bf16[384,1024]{1,0:T(8,128)(2,1)S(1)}, bf16[384,1024]{1,0:T(8,128)(2,1)S(1)}, u32[]{:S(2)}, u32[]{:S(2)}) collective-permute-start(bf16[384,1024]{1,0:T(8,128)(2,1)S(1)} %copy-done.1), channel_id=1, source_target_pairs={{0,64},{1,65},{2,66},{3,67},{4,68},{5,69},{6,70},{7,71},{8,72},{9,... | collective-permute-start | bytes 2359304 | tf_op jit(solution)/shard_map/ppermute | solution.py:196

commit v3 on v2

v3 whole, which is shorter than its diff:
```python
import functools

import jax
import jax.numpy as jnp
from jax import lax
from jax.experimental import pallas as pl
from jax.experimental.pallas import tpu as pltpu
from jax.sharding import PartitionSpec as P

CODE_ROWS = 8
NO_MATCH = -256.0
VMEM_LIMIT = 32 * 1024 * 1024
LAST_ROWS = 64
BLK_1, GROUP_1, BLK_2, OWN = range(4)


def units_of(values):
    wide = values.astype(jnp.float32)
    scale = lax.rsqrt(jnp.sum(wide * wide, axis=-1, keepdims=True) + 1e-06)
    return wide * scale, scale


def codes_of(ints, partner):
    rows = partner.shape[1]
    row = lax.broadcasted_iota(jnp.int32, (CODE_ROWS, rows), 0)
    codes = jnp.full((CODE_ROWS, rows), NO_MATCH, jnp.float32)
    for kind in range(4):
        place = partner - ints[kind]
        inside = (place >= 0) & (place < rows)
        code = jnp.where(inside, (place - rows // 2).astype(jnp.float32), NO_MATCH)
        codes = jnp.where(row == kind, code, codes)
    return codes


def pack_kernel(flags, ints, image_ref, text_ref, partner_ref, *refs):
    out_refs, done = refs[:-1], refs[-1]
    rows, width = image_ref.shape
    for n, (flag, out_ref) in enumerate(zip(flags, out_refs)):

        def begin(ref, n=n, out_ref=out_ref):
            pltpu.make_async_copy(ref, out_ref.at[:rows, :], done.at[n]).start()

        if flag is None:
            begin(image_ref)
        else:
            pl.when(ints[flag] != 0)(lambda begin=begin: begin(image_ref))
            pl.when(ints[flag] == 0)(lambda begin=begin: begin(text_ref))
    codes = codes_of(ints, partner_ref[...].reshape(1, rows))
    for out_ref in out_refs:
        out_ref[rows:, :rows] = codes.astype(out_ref.dtype)
        out_ref[rows:, rows:] = jnp.zeros((CODE_ROWS, width - rows), out_ref.dtype)
    for n, out_ref in enumerate(out_refs):
        pltpu.make_async_copy(image_ref, out_ref.at[:rows, :], done.at[n]).wait()


def pack(flags, ints, image, text, partner):
    rows, width = image.shape
    vmem, given = pl.BlockSpec(memory_space=pltpu.VMEM), pl.BlockSpec(memory_space=pl.ANY)
    return pl.pallas_call(
        functools.partial(pack_kernel, flags),
        out_shape=[jax.ShapeDtypeStruct((rows + CODE_ROWS, width), jnp.bfloat16)] * len(flags),
        in_specs=[pl.BlockSpec(memory_space=pltpu.SMEM), given, given, vmem],
        out_specs=[vmem] * len(flags),
        scratch_shapes=[pltpu.SemaphoreType.DMA((len(flags),))],
        compiler_params=pltpu.CompilerParams(vmem_limit_bytes=VMEM_LIMIT),
        cost_estimate=pl.CostEstimate(
            flops=rows * width, bytes_accessed=4 * len(flags) * rows * width, transcendentals=0
        ),
    )(ints, image, text, partner)


def term(side, kind, ints, floats, unit, foreign_refs, picks, partner_ref):
    rows = unit.shape[0]
    block = foreign_refs[0][...]
    for other_ref, flag in zip(foreign_refs[1:], picks):
        block = jnp.where(ints[flag] != 0, other_ref[...], block)
    foreign = units_of(block[:rows, :])[0].astype(jnp.bfloat16)
    scores = (
        floats[0]
        * lax.dot_general(
            unit.astype(jnp.bfloat16),
            foreign,
            (((1,), (1,)), ((), ())),
            preferred_element_type=jnp.float32,
        )
        + floats[1]
    )
    if side == "image":
        columns = ints[kind] + lax.broadcasted_iota(jnp.int32, scores.shape, 1)
        matches = partner_ref[...] == columns
    else:
        code = block[rows:, :rows].astype(jnp.float32)[kind : kind + 1, :]
        place = lax.broadcasted_iota(jnp.int32, scores.shape, 0) - rows // 2
        matches = place.astype(jnp.float32) == code
    slope = jax.nn.sigmoid(jnp.where(matches, -scores, scores))
    signal = jnp.where(matches, -slope, slope).astype(jnp.bfloat16)
    return jnp.dot(signal, foreign, preferred_element_type=jnp.float32)


def finish(floats, own_ref, sum_ref, held, out_ref, done):
    copies = []
    for n, start in enumerate(range(0, own_ref.shape[0], LAST_ROWS)):
        here = slice(start, start + LAST_ROWS)
        unit, scale = units_of(own_ref[here, :])
        part = floats[0] * sum_ref[here, :]
        along = jnp.sum(unit * part, axis=-1, keepdims=True)
        held[here, :] = (part - unit * along) * scale
        copies.append(pltpu.make_async_copy(held.at[here, :], out_ref.at[here, :], done.at[n]))
        copies[-1].start()
    for copy in copies:
        copy.wait()


def early_kernel(odd, ints, floats, image, text, partner, packed, x_text, x_image, chip, image_sum, text_sum):
    image_unit, text_unit = units_of(image[...])[0], units_of(text[...])[0]
    image_sum[...] = term("image", OWN, ints, floats, image_unit, [text], (), partner)
    image_sum[...] += term("image", BLK_2, ints, floats, image_unit, [x_text], (), partner)
    text_sum[...] = term("text", OWN, ints, floats, text_unit, [packed], (), partner)
    text_sum[...] += term("text", BLK_2, ints, floats, text_unit, [x_image], (), partner)

    @pl.when(ints[odd] != 0)
    def _():
        image_sum[...] += term("image", GROUP_1, ints, floats, image_unit, [chip], (), partner)

    @pl.when(ints[odd] == 0)
    def _():
        text_sum[...] += term("text", GROUP_1, ints, floats, text_unit, [chip], (), partner)


def middle_kernel(
    odd, first, ints, floats, image, text, partner, image_so_far, text_so_far, early, late,
    image_sum, text_sum, image_grad, text_grad, held, done,
):
    image_unit, text_unit = units_of(image[...])[0], units_of(text[...])[0]

    def image_term():
        more = term("image", BLK_1, ints, floats, image_unit, [early, late], (first,), partner)
        image_sum[...] = image_so_far[...] + more

    def text_term():
        more = term("text", BLK_1, ints, floats, text_unit, [late, early], (first,), partner)
        text_sum[...] = text_so_far[...] + more

    image_term()
    text_term()

    @pl.when(ints[odd] != 0)
    def _():
        finish(floats, image, image_sum, held, image_grad, done)

    @pl.when(ints[odd] == 0)
    def _():
        finish(floats, text, text_sum, held, text_grad, done)


def last_kernel(
    odd, first, final, ints, floats, image, text, partner, image_so_far, text_so_far, link, handed,
    image_done, text_done, image_grad, text_grad, total, held, done,
):
    @pl.when(ints[odd] != 0)
    def _():
        unit = units_of(text[...])[0]
        more = term("text", GROUP_1, ints, floats, unit, [link, handed], (final,), partner)
        total[...] = text_so_far[...] + more
        finish(floats, text, total, held, text_grad, done)

    @pl.when(ints[odd] == 0)
    def _():
        unit = units_of(image[...])[0]
        more = term("image", GROUP_1, ints, floats, unit, [link, handed], (first,), partner)
        total[...] = image_so_far[...] + more
        finish(floats, image, total, held, image_grad, done)


def call(kernel, terms, sums, grads, held, ints, floats, *args, aliased=0):
    rows, width = args[0].shape
    vmem, given = pl.BlockSpec(memory_space=pltpu.VMEM), pl.BlockSpec(memory_space=pl.ANY)
    shape = jax.ShapeDtypeStruct((rows, width), jnp.float32)
    plain = len(args) - aliased
    return pl.pallas_call(
        kernel,
        out_shape=[shape] * (sums + grads),
        in_specs=[pl.BlockSpec(memory_space=pltpu.SMEM)] * 2 + [vmem] * plain + [given] * aliased,
        out_specs=[vmem] * sums + [given] * grads,
        input_output_aliases={2 + plain + n: n for n in range(aliased)},
        scratch_shapes=[pltpu.VMEM((rows, width), jnp.float32)] * held
        + ([pltpu.SemaphoreType.DMA((rows // LAST_ROWS,))] if held else []),
        compiler_params=pltpu.CompilerParams(vmem_limit_bytes=VMEM_LIMIT),
        cost_estimate=pl.CostEstimate(
            flops=4 * terms * rows * rows * width,
            bytes_accessed=12 * terms * rows * width,
            transcendentals=terms * rows * rows,
        ),
    )(ints, floats, *args)


def per_device(image_embed, text_embed, partner, exponent_of_multiplier, logit_bias):
    floats = jnp.concatenate([jnp.exp(exponent_of_multiplier), logit_bias])
    cycle = lax.axis_size("blk")
    groups = lax.axis_size("group")
    rows = image_embed.shape[0]
    g = lax.axis_index("group")
    b = lax.axis_index("blk")

    def send(array, target):
        pairs = []
        for i in range(groups):
            for j in range(cycle):
                to = target(i, j)
                if to is not None:
                    pairs.append((i * cycle + j, (to[0] % groups) * cycle + to[1] % cycle))
        return lax.ppermute(array, ("group", "blk"), pairs)

    def first_of(group_at, cycle_at):
        return (group_at * cycle + cycle_at) * rows

    text_first = [
        first_of(g, (b + cycle - 1) % cycle),
        first_of((g + groups - 1) % groups, b),
        first_of(g, (b + cycle - 2) % cycle),
        first_of(g, b),
    ]
    is_first_group = g == 0
    flags = [is_first_group, g != 0, g % 2 == 1, g % 2 == 0, g == groups - 1]
    ints = jnp.stack(text_first + [flag.astype(jnp.int32) for flag in flags])
    is_first, not_first, is_odd, is_even, is_last = range(4, 9)

    codes = codes_of(text_first, partner[None, :])
    codes = jnp.pad(codes.astype(jnp.bfloat16), ((0, 0), (0, image_embed.shape[1] - rows)))
    early = jnp.concatenate([jnp.where(is_first_group, image_embed, text_embed), codes])
    early, image_again, text_again = lax.optimization_barrier((early, image_embed, text_embed))
    early_in = send(early, lambda i, j: (i, j - 1) if i == 0 else (i, j + 1))
    late, link, chip, packed = pack(
        (not_first, is_even, is_odd, None), ints, image_again, text_again, partner
    )
    x_text = send(text_again, lambda i, j: (i, j + 2))
    x_image = send(packed, lambda i, j: (i, j - 2))
    late_in = send(late, lambda i, j: (i, j + 1) if i == 0 else (i, j - 1))
    link, early_in = lax.optimization_barrier((link, early_in))
    chip_in = send(chip, lambda i, j: (i ^ 1, j))
    link_in = send(
        link, lambda i, j: None if i in (0, groups - 1) else (i + 1, j) if i % 2 else (i - 1, j)
    )
    handed = send(
        early_in,
        lambda i, j: (groups - 1, j + 1) if i == 0 else (0, j - 1) if i == groups - 1 else None,
    )

    own = (image_embed, text_embed, partner[:, None])
    kernel = functools.partial(early_kernel, is_odd)
    so_far = call(kernel, 5, 2, 0, 0, ints, floats, *own, packed, x_text, x_image, chip_in)
    kernel = functools.partial(middle_kernel, is_odd, is_first)
    *so_far, image_grad, text_grad = call(
        kernel, 2, 2, 2, 1, ints, floats, *own, *so_far, early_in, late_in
    )
    kernel = functools.partial(last_kernel, is_odd, is_first, is_last)
    return call(
        kernel, 1, 0, 2, 2, ints, floats, *own, *so_far, link_in, handed, image_grad, text_grad, aliased=2
    )


def solution(mesh):
    return jax.shard_map(
        per_device,
        mesh=mesh,
        in_specs=(
            P(("group", "blk"), None),
            P(("group", "blk"), None),
            P(("group", "blk")),
            P(),
            P(),
        ),
        out_specs=(P(("group", "blk"), None), P(("group", "blk"), None)),
        check_vma=False,
    )
```

time: 142 us -> 137 us (0.965)
  waiting for transfers between devices: 40.2 us -> 29.5 us
  starting transfers between devices: 81.7 us -> 86.9 us
  local copies, waits for them, and re-layouts: 3.14 us -> 0.21 us
  other arithmetic: 0.08 us -> 2.46 us
    ppermute x7, waiting for transfers between devices: 40.2 us -> 29.5 us  [send(): return lax.ppermute(array, ('group', 'blk'), pairs)]
    ppermute x7, starting transfers between devices: 81.7 us -> 86.9 us  [send(): return lax.ppermute(array, ('group', 'blk'), pairs)]
    unnamed x6, local copies, waits for them, and re-layouts: 2.95 us -> 0.02 us
    pallas_call x5 -> x4, Pallas kernels: 14.2 us -> 15.6 us  [the longest x3 14.8 us: call(): pl.pallas_call(kernel, out_shape=[shape] * (sums + grads), in_specs=[pl.B...]
  transfers between devices with their start and end apart: 7 -> 7, of which waited for: 4 -> 2; matrix products, arithmetic and copies ran while one was open for 0% -> 0% of each run, Pallas kernels for 6% -> 9%
where the time goes in v3:
time: 137 us
  starting transfers between devices  86.9 us (63%)
  waiting for transfers between devices  29.5 us (22%)
  Pallas kernels  15.6 us (11%)
  other arithmetic  2.46 us (2%)
  between operations  2.41 us (2%)
    ppermute x7, starting transfers between devices, send(): return lax.ppermute(array, ('group', 'blk'), pairs)  86.9 us
    ppermute x7, waiting for transfers between devices, send(): return lax.ppermute(array, ('group', 'blk'), pairs)  29.5 us
    pallas_call x3, Pallas kernels, call(): pl.pallas_call(kernel, out_shape=[shape] * (sums + grads), in_specs=[pl.B...  14.8 us
  transfers between devices with their start and end apart: 7, of which 2 were waited for; matrix products, arithmetic and copies ran while one was open for 0% of the time, Pallas kernels for 9%

profile of v3, /device:TPU:1, one launch (start us, length us, event | category | flops | bytes accessed | tf_op | source)
XLA Modules:
  0.0 137.1 jit_solution(2210016283852080106)
XLA Ops:
  0.6 0.0 copy-start.2
  0.7 0.0 copy-start.1
  0.8 0.0 copy-start
  0.8 1.3 broadcast_select_fusion
  2.1 0.0 copy-done.2
  2.1 0.1 select_convert_fusion
  2.2 0.9 fusion.1
  3.2 15.7 %collective-permute-start.3 = (bf16[392,1024]{1,0:T(8,128)(2,1)}, bf16[392,1024]{1,0:T(8,128)(2,1)S(1)}, u32[]{:S(2)}, u32[]{:S(2)}) collective-permute-start(bf16[392,1024]{1,0:T(8,128)(2,1)} %fusion.1), channel_id=1, source_target_pairs={{0,63},{1,0},{2,1},{3,2},{4,3},{5,4},{6,5},{7,6},{8,7},{9,8},{10,9... | collective-permute-start | bytes 2408456 | tf_op jit(solution)/shard_map/ppermute | solution.py:212
  18.9 0.0 copy-done.1
  18.9 3.1 %collective-permute-start = (bf16[384,1024]{1,0:T(8,128)(2,1)S(1)}, bf16[384,1024]{1,0:T(8,128)(2,1)S(1)}, u32[]{:S(2)}, u32[]{:S(2)}) collective-permute-start(bf16[384,1024]{1,0:T(8,128)(2,1)S(1)} %copy-done.1), channel_id=1, source_target_pairs={{0,2},{1,3},{2,4},{3,5},{4,6},{5,7},{6,8},{7,9},{8,10},{9,11},{10,... | collective-permute-start | bytes 2359304 | tf_op jit(solution)/shard_map/ppermute | solution.py:212
  22.0 0.1 stack.59.ints
  22.1 0.0 copy-done
  22.1 0.9 shard_map.68
  23.0 6.1 %collective-permute-start.1 = (bf16[392,1024]{1,0:T(8,128)(2,1)S(1)}, bf16[392,1024]{1,0:T(8,128)(2,1)S(1)}, u32[]{:S(2)}, u32[]{:S(2)}) collective-permute-start(bf16[392,1024]{1,0:T(8,128)(2,1)S(1)} %get-tuple-element.19.packed), channel_id=1, source_target_pairs={{0,62},{1,63},{2,0},{3,1},{4,2},{5,3},{6,4},{7,5},{8,6},{9,7},{10,... | collective-permute-start | bytes 2408456 | tf_op jit(solution)/shard_map/ppermute | solution.py:212
  29.1 7.9 %collective-permute-start.2 = (bf16[392,1024]{1,0:T(8,128)(2,1)S(1)}, bf16[392,1024]{1,0:T(8,128)(2,1)S(1)}, u32[]{:S(2)}, u32[]{:S(2)}) collective-permute-start(bf16[392,1024]{1,0:T(8,128)(2,1)S(1)} %get-tuple-element.20), channel_id=1, source_target_pairs={{0,64},{1,65},{2,66},{3,67},{4,68},{5,69},{6,70},{7,71},{8,72},{9,... | collective-permute-start | bytes 2408456 | tf_op jit(solution)/shard_map/ppermute | solution.py:212
  37.0 1.9 %collective-permute-start.4 = (bf16[392,1024]{1,0:T(8,128)(2,1)S(1)}, bf16[392,1024]{1,0:T(8,128)(2,1)S(1)}, u32[]{:S(2)}, u32[]{:S(2)}) collective-permute-start(bf16[392,1024]{1,0:T(8,128)(2,1)S(1)} %get-tuple-element.26), channel_id=1, source_target_pairs={{0,1},{1,2},{2,3},{3,4},{4,5},{5,6},{6,7},{7,8},{8,9},{9,10},{10,1... | collective-permute-start | bytes 2408456 | tf_op jit(solution)/shard_map/ppermute | solution.py:212
  38.9 4.3 %collective-permute-done.3.early = bf16[392,1024]{1,0:T(8,128)(2,1)S(1)} collective-permute-done((bf16[392,1024]{1,0:T(8,128)(2,1)}, bf16[392,1024]{1,0:T(8,128)(2,1)S(1)}, u32[]{:S(2)}, u32[]{:S(2)}) %collective-permute-start.3) | collective-permute-done | bytes 802848 | tf_op jit(solution)/shard_map/ppermute | solution.py:212
  43.2 51.5 %collective-permute-start.5 = (bf16[392,1024]{1,0:T(8,128)(2,1)S(1)}, bf16[392,1024]{1,0:T(8,128)(2,1)S(1)}, u32[]{:S(2)}, u32[]{:S(2)}) collective-permute-start(bf16[392,1024]{1,0:T(8,128)(2,1)S(1)} %get-tuple-element.29), channel_id=1, source_target_pairs={{64,128},{65,129},{66,130},{67,131},{68,132},{69,133},{70,134},{71... | collective-permute-start | bytes 2408456 | tf_op jit(solution)/shard_map/ppermute | solution.py:212
  94.6 0.0 collective-permute-done.x_text
  94.7 0.7 collective-permute-start.6
  95.4 0.1 broadcast_in_dim.44.partner
  96.8 0.1 pad_maximum_fusion.floats
  96.9 0.0 collective-permute-done.1.x_image
  96.9 0.0 collective-permute-done.2.chip
  96.9 6.2 %shard_map.69 = (f32[384,1024]{1,0:T(8,128)S(1)}, f32[384,1024]{1,0:T(8,128)S(1)}) custom-call(s32[9]{0:T(128)S(1)} %stack.59.ints, f32[2]{0:T(128)S(1)} %pad_maximum_fusion.floats, bf16[384,1024]{1,0:T(8,128)(2,1)S(1)} %copy-done, bf16[384,1024]{1,0:T(8,128)(2,1)S(1)} %copy-done.1, s32[384,1]{1,0:T(8,128)S(1)} %broadcast_in_dim.44.partner, ...), custom_call_target="tpu_custom_call" | custom-call | flops 3019898880 | bytes 23592960 | tf_op jit(solution)/shard_map/pallas_call | solution.py:180
  103.1 0.0 collective-permute-done.4.late
  103.2 5.0 %shard_map.70 = (f32[384,1024]{1,0:T(8,128)S(1)}, f32[384,1024]{1,0:T(8,128)S(1)}, f32[384,1024]{1,0:T(8,128)}, f32[384,1024]{1,0:T(8,128)}) custom-call(s32[9]{0:T(128)S(1)} %stack.59.ints, f32[2]{0:T(128)S(1)} %pad_maximum_fusion.floats, bf16[384,1024]{1,0:T(8,128)(2,1)S(1)} %copy-done, bf16[384,1024]{1,0:T(8,128)(2,1)S(1)} %copy-done.1, ...), custom_call_target="tpu_custom_call" | custom-call | flops 1207959552 | bytes 9437184 | tf_op jit(solution)/shard_map/pallas_call | solution.py:180
  108.1 25.2 %collective-permute-done.5.link = bf16[392,1024]{1,0:T(8,128)(2,1)S(1)} collective-permute-done((bf16[392,1024]{1,0:T(8,128)(2,1)S(1)}, bf16[392,1024]{1,0:T(8,128)(2,1)S(1)}, u32[]{:S(2)}, u32[]{:S(2)}) %collective-permute-start.5) | collective-permute-done | bytes 802848 | tf_op jit(solution)/shard_map/ppermute | solution.py:212
  133.4 0.0 collective-permute-done.6.handed
  133.4 3.6 %shard_map.71 = (f32[384,1024]{1,0:T(8,128)}, f32[384,1024]{1,0:T(8,128)}) custom-call(s32[9]{0:T(128)S(1)} %stack.59.ints, f32[2]{0:T(128)S(1)} %pad_maximum_fusion.floats, bf16[384,1024]{1,0:T(8,128)(2,1)S(1)} %copy-done, bf16[384,1024]{1,0:T(8,128)(2,1)S(1)} %copy-done.1, ...), custom_call_target="tpu_custom_call", output_to_operand_aliasing={{0}: (9, {}), {1}: (10, {})} | custom-call | flops 603979776 | bytes 4718592 | tf_op jit(solution)/shard_map/pallas_call | solution.py:180
  (3 shorter events, 0.0 us)
Async XLA Ops:
  0.6 1.5 %copy-start.2 = (s32[384]{0:T(512)S(1)}, s32[384]{0:T(512)}, u32[]{:S(2)}) copy-start(s32[384]{0:T(512)} %partner_ref.1) | copy-start | bytes 4612
  0.7 18.1 %copy-start.1 = (bf16[384,1024]{1,0:T(8,128)(2,1)S(1)}, bf16[384,1024]{1,0:T(8,128)(2,1)}, u32[]{:S(2)}) copy-start(bf16[384,1024]{1,0:T(8,128)(2,1)} %text.5) | copy-start | bytes 2359300
  0.8 21.3 %copy-start = (bf16[384,1024]{1,0:T(8,128)(2,1)S(1)}, bf16[384,1024]{1,0:T(8,128)(2,1)}, u32[]{:S(2)}) copy-start(bf16[384,1024]{1,0:T(8,128)(2,1)} %image.5) | copy-start | bytes 2359300
  3.2 40.0 %collective-permute-start.3 = (bf16[392,1024]{1,0:T(8,128)(2,1)}, bf16[392,1024]{1,0:T(8,128)(2,1)S(1)}, u32[]{:S(2)}, u32[]{:S(2)}) collective-permute-start(bf16[392,1024]{1,0:T(8,128)(2,1)} %fusion.1), channel_id=1, source_target_pairs={{0,63},{1,0},{2,1},{3,2},{4,3},{5,4},{6,5},{7,6},{8,7},{9,8},{10,9... | collective-permute-start | bytes 2408456 | tf_op jit(solution)/shard_map/ppermute | solution.py:212
  18.9 75.8 %collective-permute-start = (bf16[384,1024]{1,0:T(8,128)(2,1)S(1)}, bf16[384,1024]{1,0:T(8,128)(2,1)S(1)}, u32[]{:S(2)}, u32[]{:S(2)}) collective-permute-start(bf16[384,1024]{1,0:T(8,128)(2,1)S(1)} %copy-done.1), channel_id=1, source_target_pairs={{0,2},{1,3},{2,4},{3,5},{4,6},{5,7},{6,8},{7,9},{8,10},{9,11},{10,... | collective-permute-start | bytes 2359304 | tf_op jit(solution)/shard_map/ppermute | solution.py:212
  23.0 73.9 %collective-permute-start.1 = (bf16[392,1024]{1,0:T(8,128)(2,1)S(1)}, bf16[392,1024]{1,0:T(8,128)(2,1)S(1)}, u32[]{:S(2)}, u32[]{:S(2)}) collective-permute-start(bf16[392,1024]{1,0:T(8,128)(2,1)S(1)} %get-tuple-element.19.packed), channel_id=1, source_target_pairs={{0,62},{1,63},{2,0},{3,1},{4,2},{5,3},{6,4},{7,5},{8,6},{9,7},{10,... | collective-permute-start | bytes 2408456 | tf_op jit(solution)/shard_map/ppermute | solution.py:212
  29.1 67.8 %collective-permute-start.2 = (bf16[392,1024]{1,0:T(8,128)(2,1)S(1)}, bf16[392,1024]{1,0:T(8,128)(2,1)S(1)}, u32[]{:S(2)}, u32[]{:S(2)}) collective-permute-start(bf16[392,1024]{1,0:T(8,128)(2,1)S(1)} %get-tuple-element.20), channel_id=1, source_target_pairs={{0,64},{1,65},{2,66},{3,67},{4,68},{5,69},{6,70},{7,71},{8,72},{9,... | collective-permute-start | bytes 2408456 | tf_op jit(solution)/shard_map/ppermute | solution.py:212
  37.0 66.2 %collective-permute-start.4 = (bf16[392,1024]{1,0:T(8,128)(2,1)S(1)}, bf16[392,1024]{1,0:T(8,128)(2,1)S(1)}, u32[]{:S(2)}, u32[]{:S(2)}) collective-permute-start(bf16[392,1024]{1,0:T(8,128)(2,1)S(1)} %get-tuple-element.26), channel_id=1, source_target_pairs={{0,1},{1,2},{2,3},{3,4},{4,5},{5,6},{6,7},{7,8},{8,9},{9,10},{10,1... | collective-permute-start | bytes 2408456 | tf_op jit(solution)/shard_map/ppermute | solution.py:212
  43.2 90.2 %collective-permute-start.5 = (bf16[392,1024]{1,0:T(8,128)(2,1)S(1)}, bf16[392,1024]{1,0:T(8,128)(2,1)S(1)}, u32[]{:S(2)}, u32[]{:S(2)}) collective-permute-start(bf16[392,1024]{1,0:T(8,128)(2,1)S(1)} %get-tuple-element.29), channel_id=1, source_target_pairs={{64,128},{65,129},{66,130},{67,131},{68,132},{69,133},{70,134},{71... | collective-permute-start | bytes 2408456 | tf_op jit(solution)/shard_map/ppermute | solution.py:212
  94.7 38.7 %collective-permute-start.6 = (bf16[392,1024]{1,0:T(8,128)(2,1)S(1)}, bf16[392,1024]{1,0:T(8,128)(2,1)S(1)}, u32[]{:S(2)}, u32[]{:S(2)}) collective-permute-start(bf16[392,1024]{1,0:T(8,128)(2,1)S(1)} %collective-permute-done.3.early), channel_id=1, source_target_pairs={{0,705},{1,706},{2,707},{3,708},{4,709},{5,710},{6,711},{7,712},{8... | collective-permute-start | bytes 2408456 | tf_op jit(solution)/shard_map/ppermute | solution.py:212

commit v4 on v3

--- a/solution.py
+++ b/solution.py
@@ -71,9 +71,10 @@
 
 def term(side, kind, ints, floats, unit, foreign_refs, picks, partner_ref):
     rows = unit.shape[0]
-    block = foreign_refs[0][...]
+    height = rows if side == "image" else rows + CODE_ROWS
+    block = foreign_refs[0][:height, :]
     for other_ref, flag in zip(foreign_refs[1:], picks):
-        block = jnp.where(ints[flag] != 0, other_ref[...], block)
+        block = jnp.where(ints[flag] != 0, other_ref[:height, :], block)
     foreign = units_of(block[:rows, :])[0].astype(jnp.bfloat16)
     scores = (
         floats[0]
@@ -111,45 +112,40 @@
         copy.wait()
 
 
-def early_kernel(odd, ints, floats, image, text, partner, packed, x_text, x_image, chip, image_sum, text_sum):
+def own_kernel(ints, floats, image, text, partner, packed, image_sum, text_sum):
     image_unit, text_unit = units_of(image[...])[0], units_of(text[...])[0]
     image_sum[...] = term("image", OWN, ints, floats, image_unit, [text], (), partner)
-    image_sum[...] += term("image", BLK_2, ints, floats, image_unit, [x_text], (), partner)
     text_sum[...] = term("text", OWN, ints, floats, text_unit, [packed], (), partner)
-    text_sum[...] += term("text", BLK_2, ints, floats, text_unit, [x_image], (), partner)
-
-    @pl.when(ints[odd] != 0)
-    def _():
-        image_sum[...] += term("image", GROUP_1, ints, floats, image_unit, [chip], (), partner)
-
-    @pl.when(ints[odd] == 0)
-    def _():
-        text_sum[...] += term("text", GROUP_1, ints, floats, text_unit, [chip], (), partner)
+
+
+def x_kernel(
+    ints, floats, image, text, partner, image_so_far, text_so_far, x_text, x_image, image_sum, text_sum
+):
+    image_unit, text_unit = units_of(image[...])[0], units_of(text[...])[0]
+    more = term("image", BLK_2, ints, floats, image_unit, [x_text], (), partner)
+    image_sum[...] = image_so_far[...] + more
+    more = term("text", BLK_2, ints, floats, text_unit, [x_image], (), partner)
+    text_sum[...] = text_so_far[...] + more
 
 
 def middle_kernel(
-    odd, first, ints, floats, image, text, partner, image_so_far, text_so_far, early, late,
+    odd, first, ints, floats, image, text, partner, image_so_far, text_so_far, early_text, early_image, late, chip,
     image_sum, text_sum, image_grad, text_grad, held, done,
 ):
     image_unit, text_unit = units_of(image[...])[0], units_of(text[...])[0]
-
-    def image_term():
-        more = term("image", BLK_1, ints, floats, image_unit, [early, late], (first,), partner)
-        image_sum[...] = image_so_far[...] + more
-
-    def text_term():
-        more = term("text", BLK_1, ints, floats, text_unit, [late, early], (first,), partner)
-        text_sum[...] = text_so_far[...] + more
-
-    image_term()
-    text_term()
+    more = term("image", BLK_1, ints, floats, image_unit, [early_text, late], (first,), partner)
+    image_sum[...] = image_so_far[...] + more
+    more = term("text", BLK_1, ints, floats, text_unit, [late, early_image], (first,), partner)
+    text_sum[...] = text_so_far[...] + more
 
     @pl.when(ints[odd] != 0)
     def _():
+        image_sum[...] += term("image", GROUP_1, ints, floats, image_unit, [chip], (), partner)
         finish(floats, image, image_sum, held, image_grad, done)
 
     @pl.when(ints[odd] == 0)
     def _():
+        text_sum[...] += term("text", GROUP_1, ints, floats, text_unit, [chip], (), partner)
         finish(floats, text, text_sum, held, text_grad, done)
 
 
@@ -225,33 +221,31 @@
     ints = jnp.stack(text_first + [flag.astype(jnp.int32) for flag in flags])
     is_first, not_first, is_odd, is_even, is_last = range(4, 9)
 
-    codes = codes_of(text_first, partner[None, :])
-    codes = jnp.pad(codes.astype(jnp.bfloat16), ((0, 0), (0, image_embed.shape[1] - rows)))
-    early = jnp.concatenate([jnp.where(is_first_group, image_embed, text_embed), codes])
-    early, image_again, text_again = lax.optimization_barrier((early, image_embed, text_embed))
-    early_in = send(early, lambda i, j: (i, j - 1) if i == 0 else (i, j + 1))
+    early_text = send(text_embed, lambda i, j: None if i == 0 else (i, j + 1))
     late, link, chip, packed = pack(
-        (not_first, is_even, is_odd, None), ints, image_again, text_again, partner
-    )
+        (not_first, is_even, is_odd, None), ints, image_embed, text_embed, partner
+    )
+    early_image = send(packed, lambda i, j: (i, j - 1) if i == 0 else None)
+    packed_again, text_again = lax.optimization_barrier((packed, text_embed))
     x_text = send(text_again, lambda i, j: (i, j + 2))
-    x_image = send(packed, lambda i, j: (i, j - 2))
+    x_image = send(packed_again, lambda i, j: (i, j - 2))
     late_in = send(late, lambda i, j: (i, j + 1) if i == 0 else (i, j - 1))
-    link, early_in = lax.optimization_barrier((link, early_in))
+    link, chip, early_text, ints_later = lax.optimization_barrier((link, chip, early_text, ints))
     chip_in = send(chip, lambda i, j: (i ^ 1, j))
     link_in = send(
         link, lambda i, j: None if i in (0, groups - 1) else (i + 1, j) if i % 2 else (i - 1, j)
     )
+    own = (image_embed, text_embed, partner[:, None])
+    so_far = call(own_kernel, 2, 2, 0, 0, ints_later, floats, *own, packed)
+    early_image, *so_far = lax.optimization_barrier((early_image, *so_far))
+    so_far = call(x_kernel, 2, 2, 0, 0, ints, floats, *own, *so_far, x_text, x_image)
     handed = send(
-        early_in,
+        jnp.where(is_first_group, early_image, jnp.pad(early_text, ((0, CODE_ROWS), (0, 0)))),
         lambda i, j: (groups - 1, j + 1) if i == 0 else (0, j - 1) if i == groups - 1 else None,
     )
-
-    own = (image_embed, text_embed, partner[:, None])
-    kernel = functools.partial(early_kernel, is_odd)
-    so_far = call(kernel, 5, 2, 0, 0, ints, floats, *own, packed, x_text, x_image, chip_in)
     kernel = functools.partial(middle_kernel, is_odd, is_first)
     *so_far, image_grad, text_grad = call(
-        kernel, 2, 2, 2, 1, ints, floats, *own, *so_far, early_in, late_in
+        kernel, 3, 2, 2, 1, ints, floats, *own, *so_far, early_text, early_image, late_in, chip_in
     )
     kernel = functools.partial(last_kernel, is_odd, is_first, is_last)
     return call(

time: 137 us -> 134 us (0.978)
  waiting for transfers between devices: 29.5 us -> 23.5 us
  local copies, waits for them, and re-layouts: 0.21 us -> 3.14 us
  other arithmetic: 2.46 us -> 0.38 us
    ppermute x7 -> x8, waiting for transfers between devices: 29.5 us -> 23.5 us  [send(): return lax.ppermute(array, ('group', 'blk'), pairs)]
    unnamed x6, local copies, waits for them, and re-layouts: 0.02 us -> 2.95 us
    pallas_call x3 -> x4, Pallas kernels: 14.8 us -> 15.6 us  [call(): pl.pallas_call(kernel, out_shape=[shape] * (sums + grads), in_specs=[pl.B...]
    ppermute x7 -> x8, starting transfers between devices: 86.9 us -> 87.6 us  [send(): return lax.ppermute(array, ('group', 'blk'), pairs)]
  transfers between devices with their start and end apart: 7 -> 8, of which waited for: 2 -> 2; matrix products, arithmetic and copies ran while one was open for 0% -> 0% of each run, Pallas kernels for 9% -> 10%
where the time goes in v4:
time: 134 us; the launch traced here: 133 us
  starting transfers between devices  87.6 us (65%)
  waiting for transfers between devices  23.5 us (18%)
  Pallas kernels  16.5 us (12%)
  local copies, waits for them, and re-layouts  3.14 us (2%)
  between operations  2.36 us (2%)
    ppermute x8, starting transfers between devices, send(): return lax.ppermute(array, ('group', 'blk'), pairs)  87.6 us
    ppermute x8, waiting for transfers between devices, send(): return lax.ppermute(array, ('group', 'blk'), pairs)  23.5 us
    pallas_call x4, Pallas kernels, call(): pl.pallas_call(kernel, out_shape=[shape] * (sums + grads), in_specs=[pl.B...  15.6 us
    unnamed x6, local copies, waits for them, and re-layouts  2.95 us
  transfers between devices with their start and end apart: 8, of which 2 were waited for; matrix products, arithmetic and copies ran while one was open for 0% of the time, Pallas kernels for 10%

profile of v4, /device:TPU:1, one launch (start us, length us, event | category | flops | bytes accessed | tf_op | source)
XLA Modules:
  0.0 133.5 jit_solution(17335456213562445803)
XLA Ops:
  0.6 15.7 %collective-permute-start.1 = (bf16[384,1024]{1,0:T(8,128)(2,1)}, bf16[384,1024]{1,0:T(8,128)(2,1)S(1)}, u32[]{:S(2)}, u32[]{:S(2)}) collective-permute-start(bf16[384,1024]{1,0:T(8,128)(2,1)} %text.7), channel_id=1, source_target_pairs={{64,65},{65,66},{66,67},{67,68},{68,69},{69,70},{70,71},{71,72},{7... | collective-permute-start | bytes 2359304 | tf_op jit(solution)/shard_map/ppermute | solution.py:208
  16.4 0.1 stack.59.ints
  16.5 0.0 copy-start
  16.5 1.1 copy-done
  17.6 0.0 copy-start.1
  17.6 1.1 copy-done.1
  18.8 0.0 copy-start.2
  18.8 0.7 copy-done.2
  19.4 0.9 shard_map.68
  20.3 0.7 collective-permute-start
  21.0 3.1 %collective-permute-start.2 = (bf16[384,1024]{1,0:T(8,128)(2,1)S(1)}, bf16[384,1024]{1,0:T(8,128)(2,1)S(1)}, u32[]{:S(2)}, u32[]{:S(2)}) collective-permute-start(bf16[384,1024]{1,0:T(8,128)(2,1)S(1)} %copy-done.1), channel_id=1, source_target_pairs={{0,2},{1,3},{2,4},{3,5},{4,6},{5,7},{6,8},{7,9},{8,10},{9,11},{10,... | collective-permute-start | bytes 2359304 | tf_op jit(solution)/shard_map/ppermute | solution.py:208
  24.1 6.1 %collective-permute-start.3 = (bf16[392,1024]{1,0:T(8,128)(2,1)S(1)}, bf16[392,1024]{1,0:T(8,128)(2,1)S(1)}, u32[]{:S(2)}, u32[]{:S(2)}) collective-permute-start(bf16[392,1024]{1,0:T(8,128)(2,1)S(1)} %get-tuple-element.32.packed), channel_id=1, source_target_pairs={{0,62},{1,63},{2,0},{3,1},{4,2},{5,3},{6,4},{7,5},{8,6},{9,7},{10,... | collective-permute-start | bytes 2408456 | tf_op jit(solution)/shard_map/ppermute | solution.py:208
  30.2 3.1 %collective-permute-start.4 = (bf16[392,1024]{1,0:T(8,128)(2,1)S(1)}, bf16[392,1024]{1,0:T(8,128)(2,1)S(1)}, u32[]{:S(2)}, u32[]{:S(2)}) collective-permute-start(bf16[392,1024]{1,0:T(8,128)(2,1)S(1)} %get-tuple-element.37), channel_id=1, source_target_pairs={{0,1},{1,2},{2,3},{3,4},{4,5},{5,6},{6,7},{7,8},{8,9},{9,10},{10,1... | collective-permute-start | bytes 2408456 | tf_op jit(solution)/shard_map/ppermute | solution.py:208
  33.3 0.1 broadcast_in_dim.4.partner
  34.8 0.1 pad_maximum_fusion.floats
  34.9 0.1 collective-permute-done.1.early_text
  35.0 6.7 %collective-permute-start.5 = (bf16[392,1024]{1,0:T(8,128)(2,1)S(1)}, bf16[392,1024]{1,0:T(8,128)(2,1)S(1)}, u32[]{:S(2)}, u32[]{:S(2)}) collective-permute-start(bf16[392,1024]{1,0:T(8,128)(2,1)S(1)} %get-tuple-element.38), channel_id=1, source_target_pairs={{0,64},{1,65},{2,66},{3,67},{4,68},{5,69},{6,70},{7,71},{8,72},{9,... | collective-permute-start | bytes 2408456 | tf_op jit(solution)/shard_map/ppermute | solution.py:208
  41.6 2.9 %shard_map.69 = (f32[384,1024]{1,0:T(8,128)S(1)}, f32[384,1024]{1,0:T(8,128)S(1)}) custom-call(s32[9]{0:T(128)S(1)} %stack.59.ints, f32[2]{0:T(128)S(1)} %pad_maximum_fusion.floats, bf16[384,1024]{1,0:T(8,128)(2,1)S(1)} %copy-done, bf16[384,1024]{1,0:T(8,128)(2,1)S(1)} %copy-done.1, s32[384,1]{1,0:T(8,128)S(1)} %broadcast_in_dim.4.partner, ...), custom_call_target="tpu_custom_call" | custom-call | flops 1207959552 | bytes 9437184 | tf_op jit(solution)/shard_map/pallas_call | solution.py:176
  44.6 0.0 collective-permute-done.early_image
  44.6 51.5 %collective-permute-start.6 = (bf16[392,1024]{1,0:T(8,128)(2,1)S(1)}, bf16[392,1024]{1,0:T(8,128)(2,1)S(1)}, u32[]{:S(2)}, u32[]{:S(2)}) collective-permute-start(bf16[392,1024]{1,0:T(8,128)(2,1)S(1)} %get-tuple-element.41), channel_id=1, source_target_pairs={{64,128},{65,129},{66,130},{67,131},{68,132},{69,133},{70,134},{71... | collective-permute-start | bytes 2408456 | tf_op jit(solution)/shard_map/ppermute | solution.py:208
  96.1 0.3 pad_select_fusion
  96.4 0.0 collective-permute-done.2.x_text
  96.4 0.7 collective-permute-start.7
  97.2 0.0 collective-permute-done.3.x_image
  97.2 3.2 %shard_map.70 = (f32[384,1024]{1,0:T(8,128)S(1)}, f32[384,1024]{1,0:T(8,128)S(1)}) custom-call(s32[9]{0:T(128)S(1)} %stack.59.ints, f32[2]{0:T(128)S(1)} %pad_maximum_fusion.floats, bf16[384,1024]{1,0:T(8,128)(2,1)S(1)} %copy-done, bf16[384,1024]{1,0:T(8,128)(2,1)S(1)} %copy-done.1, s32[384,1]{1,0:T(8,128)S(1)} %broadcast_in_dim.4.partner, ...), custom_call_target="tpu_custom_call" | custom-call | flops 1207959552 | bytes 9437184 | tf_op jit(solution)/shard_map/pallas_call | solution.py:176
  100.3 0.0 collective-permute-done.4.late
  100.4 0.0 collective-permute-done.5.chip
  100.4 6.0 %shard_map.71 = (f32[384,1024]{1,0:T(8,128)S(1)}, f32[384,1024]{1,0:T(8,128)S(1)}, f32[384,1024]{1,0:T(8,128)}, f32[384,1024]{1,0:T(8,128)}) custom-call(s32[9]{0:T(128)S(1)} %stack.59.ints, f32[2]{0:T(128)S(1)} %pad_maximum_fusion.floats, bf16[384,1024]{1,0:T(8,128)(2,1)S(1)} %copy-done, bf16[384,1024]{1,0:T(8,128)(2,1)S(1)} %copy-done.1, ...), custom_call_target="tpu_custom_call" | custom-call | flops 1811939328 | bytes 14155776 | tf_op jit(solution)/shard_map/pallas_call | solution.py:176
  106.3 23.4 %collective-permute-done.6.link = bf16[392,1024]{1,0:T(8,128)(2,1)S(1)} collective-permute-done((bf16[392,1024]{1,0:T(8,128)(2,1)S(1)}, bf16[392,1024]{1,0:T(8,128)(2,1)S(1)}, u32[]{:S(2)}, u32[]{:S(2)}) %collective-permute-start.6) | collective-permute-done | bytes 802848 | tf_op jit(solution)/shard_map/ppermute | solution.py:208
  129.7 0.0 collective-permute-done.7.handed
  129.7 3.6 %shard_map.72 = (f32[384,1024]{1,0:T(8,128)}, f32[384,1024]{1,0:T(8,128)}) custom-call(s32[9]{0:T(128)S(1)} %stack.59.ints, f32[2]{0:T(128)S(1)} %pad_maximum_fusion.floats, bf16[384,1024]{1,0:T(8,128)(2,1)S(1)} %copy-done, bf16[384,1024]{1,0:T(8,128)(2,1)S(1)} %copy-done.1, ...), custom_call_target="tpu_custom_call", output_to_operand_aliasing={{0}: (9, {}), {1}: (10, {})} | custom-call | flops 603979776 | bytes 4718592 | tf_op jit(solution)/shard_map/pallas_call | solution.py:176
Async XLA Ops:
  0.6 34.3 %collective-permute-start.1 = (bf16[384,1024]{1,0:T(8,128)(2,1)}, bf16[384,1024]{1,0:T(8,128)(2,1)S(1)}, u32[]{:S(2)}, u32[]{:S(2)}) collective-permute-start(bf16[384,1024]{1,0:T(8,128)(2,1)} %text.7), channel_id=1, source_target_pairs={{64,65},{65,66},{66,67},{67,68},{68,69},{69,70},{70,71},{71,72},{7... | collective-permute-start | bytes 2359304 | tf_op jit(solution)/shard_map/ppermute | solution.py:208
  16.5 1.1 copy-start
  17.6 1.1 copy-start.1
  18.8 0.7 copy-start.2
  20.3 24.3 %collective-permute-start = (bf16[392,1024]{1,0:T(8,128)(2,1)S(1)}, bf16[392,1024]{1,0:T(8,128)(2,1)S(1)}, u32[]{:S(2)}, u32[]{:S(2)}) collective-permute-start(bf16[392,1024]{1,0:T(8,128)(2,1)S(1)} %get-tuple-element.32.packed), channel_id=1, source_target_pairs={{0,63},{1,0},{2,1},{3,2},{4,3},{5,4},{6,5},{7,6},{8,7},{9,8},{10,9... | collective-permute-start | bytes 2408456 | tf_op jit(solution)/shard_map/ppermute | solution.py:208
  21.0 75.4 %collective-permute-start.2 = (bf16[384,1024]{1,0:T(8,128)(2,1)S(1)}, bf16[384,1024]{1,0:T(8,128)(2,1)S(1)}, u32[]{:S(2)}, u32[]{:S(2)}) collective-permute-start(bf16[384,1024]{1,0:T(8,128)(2,1)S(1)} %copy-done.1), channel_id=1, source_target_pairs={{0,2},{1,3},{2,4},{3,5},{4,6},{5,7},{6,8},{7,9},{8,10},{9,11},{10,... | collective-permute-start | bytes 2359304 | tf_op jit(solution)/shard_map/ppermute | solution.py:208
  24.1 73.0 %collective-permute-start.3 = (bf16[392,1024]{1,0:T(8,128)(2,1)S(1)}, bf16[392,1024]{1,0:T(8,128)(2,1)S(1)}, u32[]{:S(2)}, u32[]{:S(2)}) collective-permute-start(bf16[392,1024]{1,0:T(8,128)(2,1)S(1)} %get-tuple-element.32.packed), channel_id=1, source_target_pairs={{0,62},{1,63},{2,0},{3,1},{4,2},{5,3},{6,4},{7,5},{8,6},{9,7},{10,... | collective-permute-start | bytes 2408456 | tf_op jit(solution)/shard_map/ppermute | solution.py:208
  30.2 70.1 %collective-permute-start.4 = (bf16[392,1024]{1,0:T(8,128)(2,1)S(1)}, bf16[392,1024]{1,0:T(8,128)(2,1)S(1)}, u32[]{:S(2)}, u32[]{:S(2)}) collective-permute-start(bf16[392,1024]{1,0:T(8,128)(2,1)S(1)} %get-tuple-element.37), channel_id=1, source_target_pairs={{0,1},{1,2},{2,3},{3,4},{4,5},{5,6},{6,7},{7,8},{8,9},{9,10},{10,1... | collective-permute-start | bytes 2408456 | tf_op jit(solution)/shard_map/ppermute | solution.py:208
  35.0 65.4 %collective-permute-start.5 = (bf16[392,1024]{1,0:T(8,128)(2,1)S(1)}, bf16[392,1024]{1,0:T(8,128)(2,1)S(1)}, u32[]{:S(2)}, u32[]{:S(2)}) collective-permute-start(bf16[392,1024]{1,0:T(8,128)(2,1)S(1)} %get-tuple-element.38), channel_id=1, source_target_pairs={{0,64},{1,65},{2,66},{3,67},{4,68},{5,69},{6,70},{7,71},{8,72},{9,... | collective-permute-start | bytes 2408456 | tf_op jit(solution)/shard_map/ppermute | solution.py:208
  44.6 85.2 %collective-permute-start.6 = (bf16[392,1024]{1,0:T(8,128)(2,1)S(1)}, bf16[392,1024]{1,0:T(8,128)(2,1)S(1)}, u32[]{:S(2)}, u32[]{:S(2)}) collective-permute-start(bf16[392,1024]{1,0:T(8,128)(2,1)S(1)} %get-tuple-element.41), channel_id=1, source_target_pairs={{64,128},{65,129},{66,130},{67,131},{68,132},{69,133},{70,134},{71... | collective-permute-start | bytes 2408456 | tf_op jit(solution)/shard_map/ppermute | solution.py:208
  96.4 33.3 %collective-permute-start.7 = (bf16[392,1024]{1,0:T(8,128)(2,1)S(1)}, bf16[392,1024]{1,0:T(8,128)(2,1)S(1)}, u32[]{:S(2)}, u32[]{:S(2)}) collective-permute-start(bf16[392,1024]{1,0:T(8,128)(2,1)S(1)} %pad_select_fusion), channel_id=1, source_target_pairs={{0,705},{1,706},{2,707},{3,708},{4,709},{5,710},{6,711},{7,712},{8... | collective-permute-start | bytes 2408456 | tf_op jit(solution)/shard_map/ppermute | solution.py:208

commit v5 on v4

--- a/solution.py
+++ b/solution.py
@@ -7,7 +7,7 @@
 from jax.experimental.pallas import tpu as pltpu
 from jax.sharding import PartitionSpec as P
 
-CODE_ROWS = 8
+CODE_ROWS = 16
 NO_MATCH = -256.0
 VMEM_LIMIT = 32 * 1024 * 1024
 LAST_ROWS = 64

time: 134 us -> 135 us (level)
  no operation moved by 1% of the time
where the time goes in v5:
time: 135 us
  starting transfers between devices  87.6 us (65%)
  waiting for transfers between devices  24.7 us (18%)
  Pallas kernels  16.5 us (12%)
  local copies, waits for them, and re-layouts  3.14 us (2%)
  between operations  2.36 us (2%)
    ppermute x8, starting transfers between devices, send(): return lax.ppermute(array, ('group', 'blk'), pairs)  87.6 us
    ppermute x8, waiting for transfers between devices, send(): return lax.ppermute(array, ('group', 'blk'), pairs)  24.7 us
    pallas_call x4, Pallas kernels, call(): pl.pallas_call(kernel, out_shape=[shape] * (sums + grads), in_specs=[pl.B...  15.6 us
    unnamed x6, local copies, waits for them, and re-layouts  2.95 us
  transfers between devices with their start and end apart: 8, of which 2 were waited for; matrix products, arithmetic and copies ran while one was open for 0% of the time, Pallas kernels for 10%

profile of v5, /device:TPU:1, one launch (start us, length us, event | category | flops | bytes accessed | tf_op | source)
XLA Modules:
  0.0 134.6 jit_solution(12484341454049241942)
XLA Ops:
  0.6 15.7 %collective-permute-start.1 = (bf16[384,1024]{1,0:T(8,128)(2,1)}, bf16[384,1024]{1,0:T(8,128)(2,1)S(1)}, u32[]{:S(2)}, u32[]{:S(2)}) collective-permute-start(bf16[384,1024]{1,0:T(8,128)(2,1)} %text.7), channel_id=1, source_target_pairs={{64,65},{65,66},{66,67},{67,68},{68,69},{69,70},{70,71},{71,72},{7... | collective-permute-start | bytes 2359304 | tf_op jit(solution)/shard_map/ppermute | solution.py:208
  16.4 0.1 stack.59.ints
  16.5 0.0 copy-start
  16.5 1.1 copy-done
  17.6 0.0 copy-start.1
  17.6 1.1 copy-done.1
  18.8 0.0 copy-start.2
  18.8 0.7 copy-done.2
  19.4 0.9 shard_map.68
  20.3 0.7 collective-permute-start
  21.0 3.1 %collective-permute-start.2 = (bf16[384,1024]{1,0:T(8,128)(2,1)S(1)}, bf16[384,1024]{1,0:T(8,128)(2,1)S(1)}, u32[]{:S(2)}, u32[]{:S(2)}) collective-permute-start(bf16[384,1024]{1,0:T(8,128)(2,1)S(1)} %copy-done.1), channel_id=1, source_target_pairs={{0,2},{1,3},{2,4},{3,5},{4,6},{5,7},{6,8},{7,9},{8,10},{9,11},{10,... | collective-permute-start | bytes 2359304 | tf_op jit(solution)/shard_map/ppermute | solution.py:208
  24.1 6.1 %collective-permute-start.3 = (bf16[400,1024]{1,0:T(8,128)(2,1)S(1)}, bf16[400,1024]{1,0:T(8,128)(2,1)S(1)}, u32[]{:S(2)}, u32[]{:S(2)}) collective-permute-start(bf16[400,1024]{1,0:T(8,128)(2,1)S(1)} %get-tuple-element.32.packed), channel_id=1, source_target_pairs={{0,62},{1,63},{2,0},{3,1},{4,2},{5,3},{6,4},{7,5},{8,6},{9,7},{10,... | collective-permute-start | bytes 2457608 | tf_op jit(solution)/shard_map/ppermute | solution.py:208
  30.2 3.1 %collective-permute-start.4 = (bf16[400,1024]{1,0:T(8,128)(2,1)S(1)}, bf16[400,1024]{1,0:T(8,128)(2,1)S(1)}, u32[]{:S(2)}, u32[]{:S(2)}) collective-permute-start(bf16[400,1024]{1,0:T(8,128)(2,1)S(1)} %get-tuple-element.37), channel_id=1, source_target_pairs={{0,1},{1,2},{2,3},{3,4},{4,5},{5,6},{6,7},{7,8},{8,9},{9,10},{10,1... | collective-permute-start | bytes 2457608 | tf_op jit(solution)/shard_map/ppermute | solution.py:208
  33.3 0.1 broadcast_in_dim.4.partner
  34.8 0.1 pad_maximum_fusion.floats
  34.9 0.1 collective-permute-done.1.early_text
  35.0 6.7 %collective-permute-start.5 = (bf16[400,1024]{1,0:T(8,128)(2,1)S(1)}, bf16[400,1024]{1,0:T(8,128)(2,1)S(1)}, u32[]{:S(2)}, u32[]{:S(2)}) collective-permute-start(bf16[400,1024]{1,0:T(8,128)(2,1)S(1)} %get-tuple-element.38), channel_id=1, source_target_pairs={{0,64},{1,65},{2,66},{3,67},{4,68},{5,69},{6,70},{7,71},{8,72},{9,... | collective-permute-start | bytes 2457608 | tf_op jit(solution)/shard_map/ppermute | solution.py:208
  41.6 2.9 %shard_map.69 = (f32[384,1024]{1,0:T(8,128)S(1)}, f32[384,1024]{1,0:T(8,128)S(1)}) custom-call(s32[9]{0:T(128)S(1)} %stack.59.ints, f32[2]{0:T(128)S(1)} %pad_maximum_fusion.floats, bf16[384,1024]{1,0:T(8,128)(2,1)S(1)} %copy-done, bf16[384,1024]{1,0:T(8,128)(2,1)S(1)} %copy-done.1, s32[384,1]{1,0:T(8,128)S(1)} %broadcast_in_dim.4.partner, ...), custom_call_target="tpu_custom_call" | custom-call | flops 1207959552 | bytes 9437184 | tf_op jit(solution)/shard_map/pallas_call | solution.py:176
  44.6 0.0 collective-permute-done.early_image
  44.6 51.5 %collective-permute-start.6 = (bf16[400,1024]{1,0:T(8,128)(2,1)S(1)}, bf16[400,1024]{1,0:T(8,128)(2,1)S(1)}, u32[]{:S(2)}, u32[]{:S(2)}) collective-permute-start(bf16[400,1024]{1,0:T(8,128)(2,1)S(1)} %get-tuple-element.41), channel_id=1, source_target_pairs={{64,128},{65,129},{66,130},{67,131},{68,132},{69,133},{70,134},{71... | collective-permute-start | bytes 2457608 | tf_op jit(solution)/shard_map/ppermute | solution.py:208
  96.1 0.3 pad_select_fusion
  96.4 0.0 collective-permute-done.2.x_text
  96.4 0.7 collective-permute-start.7
  97.2 0.0 collective-permute-done.3.x_image
  97.2 3.2 %shard_map.70 = (f32[384,1024]{1,0:T(8,128)S(1)}, f32[384,1024]{1,0:T(8,128)S(1)}) custom-call(s32[9]{0:T(128)S(1)} %stack.59.ints, f32[2]{0:T(128)S(1)} %pad_maximum_fusion.floats, bf16[384,1024]{1,0:T(8,128)(2,1)S(1)} %copy-done, bf16[384,1024]{1,0:T(8,128)(2,1)S(1)} %copy-done.1, s32[384,1]{1,0:T(8,128)S(1)} %broadcast_in_dim.4.partner, ...), custom_call_target="tpu_custom_call" | custom-call | flops 1207959552 | bytes 9437184 | tf_op jit(solution)/shard_map/pallas_call | solution.py:176
  100.3 0.0 collective-permute-done.4.late
  100.4 0.0 collective-permute-done.5.chip
  100.4 6.0 %shard_map.71 = (f32[384,1024]{1,0:T(8,128)S(1)}, f32[384,1024]{1,0:T(8,128)S(1)}, f32[384,1024]{1,0:T(8,128)}, f32[384,1024]{1,0:T(8,128)}) custom-call(s32[9]{0:T(128)S(1)} %stack.59.ints, f32[2]{0:T(128)S(1)} %pad_maximum_fusion.floats, bf16[384,1024]{1,0:T(8,128)(2,1)S(1)} %copy-done, bf16[384,1024]{1,0:T(8,128)(2,1)S(1)} %copy-done.1, ...), custom_call_target="tpu_custom_call" | custom-call | flops 1811939328 | bytes 14155776 | tf_op jit(solution)/shard_map/pallas_call | solution.py:176
  106.3 24.6 %collective-permute-done.6.link = bf16[400,1024]{1,0:T(8,128)(2,1)S(1)} collective-permute-done((bf16[400,1024]{1,0:T(8,128)(2,1)S(1)}, bf16[400,1024]{1,0:T(8,128)(2,1)S(1)}, u32[]{:S(2)}, u32[]{:S(2)}) %collective-permute-start.6) | collective-permute-done | bytes 819232 | tf_op jit(solution)/shard_map/ppermute | solution.py:208
  130.9 0.0 collective-permute-done.7.handed
  130.9 3.6 %shard_map.72 = (f32[384,1024]{1,0:T(8,128)}, f32[384,1024]{1,0:T(8,128)}) custom-call(s32[9]{0:T(128)S(1)} %stack.59.ints, f32[2]{0:T(128)S(1)} %pad_maximum_fusion.floats, bf16[384,1024]{1,0:T(8,128)(2,1)S(1)} %copy-done, bf16[384,1024]{1,0:T(8,128)(2,1)S(1)} %copy-done.1, ...), custom_call_target="tpu_custom_call", output_to_operand_aliasing={{0}: (9, {}), {1}: (10, {})} | custom-call | flops 603979776 | bytes 4718592 | tf_op jit(solution)/shard_map/pallas_call | solution.py:176
Async XLA Ops:
  0.6 34.3 %collective-permute-start.1 = (bf16[384,1024]{1,0:T(8,128)(2,1)}, bf16[384,1024]{1,0:T(8,128)(2,1)S(1)}, u32[]{:S(2)}, u32[]{:S(2)}) collective-permute-start(bf16[384,1024]{1,0:T(8,128)(2,1)} %text.7), channel_id=1, source_target_pairs={{64,65},{65,66},{66,67},{67,68},{68,69},{69,70},{70,71},{71,72},{7... | collective-permute-start | bytes 2359304 | tf_op jit(solution)/shard_map/ppermute | solution.py:208
  16.5 1.1 copy-start
  17.6 1.1 copy-start.1
  18.8 0.7 copy-start.2
  20.3 24.3 %collective-permute-start = (bf16[400,1024]{1,0:T(8,128)(2,1)S(1)}, bf16[400,1024]{1,0:T(8,128)(2,1)S(1)}, u32[]{:S(2)}, u32[]{:S(2)}) collective-permute-start(bf16[400,1024]{1,0:T(8,128)(2,1)S(1)} %get-tuple-element.32.packed), channel_id=1, source_target_pairs={{0,63},{1,0},{2,1},{3,2},{4,3},{5,4},{6,5},{7,6},{8,7},{9,8},{10,9... | collective-permute-start | bytes 2457608 | tf_op jit(solution)/shard_map/ppermute | solution.py:208
  21.0 75.4 %collective-permute-start.2 = (bf16[384,1024]{1,0:T(8,128)(2,1)S(1)}, bf16[384,1024]{1,0:T(8,128)(2,1)S(1)}, u32[]{:S(2)}, u32[]{:S(2)}) collective-permute-start(bf16[384,1024]{1,0:T(8,128)(2,1)S(1)} %copy-done.1), channel_id=1, source_target_pairs={{0,2},{1,3},{2,4},{3,5},{4,6},{5,7},{6,8},{7,9},{8,10},{9,11},{10,... | collective-permute-start | bytes 2359304 | tf_op jit(solution)/shard_map/ppermute | solution.py:208
  24.1 73.0 %collective-permute-start.3 = (bf16[400,1024]{1,0:T(8,128)(2,1)S(1)}, bf16[400,1024]{1,0:T(8,128)(2,1)S(1)}, u32[]{:S(2)}, u32[]{:S(2)}) collective-permute-start(bf16[400,1024]{1,0:T(8,128)(2,1)S(1)} %get-tuple-element.32.packed), channel_id=1, source_target_pairs={{0,62},{1,63},{2,0},{3,1},{4,2},{5,3},{6,4},{7,5},{8,6},{9,7},{10,... | collective-permute-start | bytes 2457608 | tf_op jit(solution)/shard_map/ppermute | solution.py:208
  30.2 70.1 %collective-permute-start.4 = (bf16[400,1024]{1,0:T(8,128)(2,1)S(1)}, bf16[400,1024]{1,0:T(8,128)(2,1)S(1)}, u32[]{:S(2)}, u32[]{:S(2)}) collective-permute-start(bf16[400,1024]{1,0:T(8,128)(2,1)S(1)} %get-tuple-element.37), channel_id=1, source_target_pairs={{0,1},{1,2},{2,3},{3,4},{4,5},{5,6},{6,7},{7,8},{8,9},{9,10},{10,1... | collective-permute-start | bytes 2457608 | tf_op jit(solution)/shard_map/ppermute | solution.py:208
  35.0 65.4 %collective-permute-start.5 = (bf16[400,1024]{1,0:T(8,128)(2,1)S(1)}, bf16[400,1024]{1,0:T(8,128)(2,1)S(1)}, u32[]{:S(2)}, u32[]{:S(2)}) collective-permute-start(bf16[400,1024]{1,0:T(8,128)(2,1)S(1)} %get-tuple-element.38), channel_id=1, source_target_pairs={{0,64},{1,65},{2,66},{3,67},{4,68},{5,69},{6,70},{7,71},{8,72},{9,... | collective-permute-start | bytes 2457608 | tf_op jit(solution)/shard_map/ppermute | solution.py:208
  44.6 86.3 %collective-permute-start.6 = (bf16[400,1024]{1,0:T(8,128)(2,1)S(1)}, bf16[400,1024]{1,0:T(8,128)(2,1)S(1)}, u32[]{:S(2)}, u32[]{:S(2)}) collective-permute-start(bf16[400,1024]{1,0:T(8,128)(2,1)S(1)} %get-tuple-element.41), channel_id=1, source_target_pairs={{64,128},{65,129},{66,130},{67,131},{68,132},{69,133},{70,134},{71... | collective-permute-start | bytes 2457608 | tf_op jit(solution)/shard_map/ppermute | solution.py:208
  96.4 34.5 %collective-permute-start.7 = (bf16[400,1024]{1,0:T(8,128)(2,1)S(1)}, bf16[400,1024]{1,0:T(8,128)(2,1)S(1)}, u32[]{:S(2)}, u32[]{:S(2)}) collective-permute-start(bf16[400,1024]{1,0:T(8,128)(2,1)S(1)} %pad_select_fusion), channel_id=1, source_target_pairs={{0,705},{1,706},{2,707},{3,708},{4,709},{5,710},{6,711},{7,712},{8... | collective-permute-start | bytes 2457608 | tf_op jit(solution)/shard_map/ppermute | solution.py:208
